TPU v7x, 128 devices: a whole 4x4x4 slice. The times are simulated.
128 devices in a mesh: grp: 4 (over y), usr: 32 (over z, x, core).
Axes of the slice: x: 4, y: 4, z: 4, core: 2. Of those that a mesh axis runs over, the one named last changes fastest.
Arguments:
- item_factors: bfloat16 [4, 1024, 128, 256], P('grp', 'usr'), may hold values from -0.29882812 to 0.29882812
- send_ids: int32 [4, 32, 32, 3], P('grp', 'usr'), may hold values from 0 to 31, as said below
- send_count: int32 [4, 32, 32], P('grp', 'usr'), may hold values from 0 to 3
- rating_pointer: int32 [4, 1792, 768], P('grp', 'usr'), may hold values from 0 to 12287
- rating_centred_value: bfloat16 [4, 1792, 768], P('grp', 'usr'), may hold values from -6 to 6
- noise: float32 [1792, 256], P('usr'), may hold values from -6 to 6
- prior_prec: float32 [256, 256], replicated, as said below
- prior_shift: float32 [256], replicated, may hold values from -6 to 6
Outputs:
- user_factors: float32 [1792, 256], P('usr')
- item_stats: float32 [4, 1024, 128, 256], P('grp', 'usr')
Inputs may be any that keep to these rules, and one draw needn't show every extreme that they name: `send_ids`: the 3 block ids of one list are distinct. `prior_prec`: symmetric with a positive diagonal larger than the sum of the magnitudes of the rest of its row.
All inputs are finite; a program needn't handle non-finite values.
Results may differ from a plain program's by a relative error of at most 0.0003.
Values may be sent and summed in bfloat16 or wider, within the bound.
A program may use at most 192 MiB of HBM per device.

v0:
```python
import jax
import jax.numpy as jnp
from jax import lax
from jax.sharding import PartitionSpec as P

ITEMS_PER_BLOCK = 128
MAX_BLOCKS_SENT = 3


ALPHA = 2.0


def tri_solve(lower, right, transpose):
    return jax.scipy.linalg.solve_triangular(lower, right, lower=True, trans=transpose)


def solve_users(gram, linear, draws, prior_prec, prior_shift):
    lower = jnp.linalg.cholesky(prior_prec[None] + ALPHA * gram)
    inner = tri_solve(lower, (ALPHA * linear + prior_shift[None])[..., None], 0)
    return tri_solve(lower, inner + draws[..., None], 1)[..., 0]


def on_device(
    item_factors,
    send_ids,
    send_count,
    rating_pointer,
    rating_centred_value,
    noise,
    prior_prec,
    prior_shift,
):
    peers = lax.axis_size("usr")
    blocks = item_factors[0]
    listed = send_ids[0, 0]
    counts = send_count[0, 0]
    rank = blocks.shape[2]
    outgoing = jnp.take(blocks, listed, axis=0)
    incoming, arrived_counts = (
        lax.all_to_all(outgoing, "usr", split_axis=0, concat_axis=0, tiled=True),
        lax.all_to_all(counts.astype(jnp.bfloat16), "usr", split_axis=0, concat_axis=0, tiled=True),
    )
    arrived_counts = arrived_counts.astype(jnp.int32)
    refs = rating_pointer[0]
    values = rating_centred_value[0]
    source = refs // (MAX_BLOCKS_SENT * ITEMS_PER_BLOCK)
    column = refs // ITEMS_PER_BLOCK % MAX_BLOCKS_SENT
    live = column < arrived_counts[source]
    flat_rows = incoming.reshape(peers * MAX_BLOCKS_SENT * ITEMS_PER_BLOCK, rank)
    rows = jnp.take(flat_rows, refs, axis=0)
    masked = jnp.where(live[..., None], rows, jnp.zeros_like(rows))
    live_value = jnp.where(live, values, jnp.zeros_like(values))
    gram = jnp.einsum("urk,url->ukl", masked, masked, preferred_element_type=jnp.float32)
    linear = jnp.einsum("ur,urk->uk", live_value, masked, preferred_element_type=jnp.float32)
    gram_part, linear_part = (
        lax.psum_scatter(gram, "grp", scatter_dimension=0, tiled=True),
        lax.psum_scatter(linear, "grp", scatter_dimension=0, tiled=True),
    )
    share = gram_part.shape[0]
    draws = lax.dynamic_slice_in_dim(noise, lax.axis_index("grp") * share, share, 0)
    own = solve_users(gram_part, linear_part, draws, prior_prec, prior_shift)
    samples = lax.all_gather(own, "grp", axis=0, tiled=True)
    weights = ALPHA * live_value.astype(jnp.float32)
    terms = weights[..., None] * samples[:, None, :]
    contrib = jax.ops.segment_sum(
        terms.reshape(-1, rank),
        refs.reshape(-1),
        num_segments=peers * MAX_BLOCKS_SENT * ITEMS_PER_BLOCK,
    )
    contrib = contrib.reshape(peers, MAX_BLOCKS_SENT, ITEMS_PER_BLOCK, rank)
    given_back = lax.all_to_all(contrib, "usr", split_axis=0, concat_axis=0, tiled=True)
    owned = blocks.shape[0]
    height = blocks.shape[1]
    stats = (
        jnp.zeros((owned, height, rank), jnp.float32)
        .at[listed.reshape(-1)]
        .add(given_back.reshape(peers * MAX_BLOCKS_SENT, height, rank))
    )
    return (samples, stats.reshape(1, owned, height, rank))


def solution(mesh):
    placed = (
        P("grp", "usr", None, None),
        P("grp", "usr", None, None),
        P("grp", "usr", None),
        P("grp", "usr", None),
        P("grp", "usr", None),
        P("usr", None),
        P(),
        P(),
    )
    return jax.shard_map(
        on_device,
        mesh=mesh,
        in_specs=placed,
        out_specs=(P("usr", None), P("grp", "usr", None, None)),
        check_vma=False,
    )
```

profile of v0, /device:TPU:1, one launch (start us, length us, event | category | flops | bytes accessed | tf_op | source)
XLA Modules:
  0.0 1909.1 jit_solution(11909704790327168025)
XLA Ops:
  8.7 9.4 all-to-all-start
  19.8 6.0 gather_fusion.1
  25.8 6.1 broadcast_select_fusion
  31.9 7.6 all-to-all-start.1
  41.0 254.3 %gather_fusion = s32[43008]{0:T(1024)S(1)} fusion(s32[32]{0:T(128)S(1)} %convert_reduce_fusion, s32[43008]{0:T(1024)S(1)} %broadcast_clamp_fusion.1), kind=kCustom, calls=%fused_computation | custom fusion | bytes 516096 | tf_op jit(solution)/shard_map/gather | solution.py:48
  295.6 162.7 %gather_fusion.2 = bf16[43008,256]{1,0:T(8,128)(2,1)} fusion(bf16[12288,256]{1,0:T(8,128)(2,1)} %bitcast.6, s32[43008]{0:T(1024)S(1)} %broadcast_clamp_fusion), kind=kCustom, calls=%fused_computation.2 | custom fusion | bytes 44212224 | tf_op jit(solution)/shard_map/jit(_take)/gather | solution.py:50
  458.3 28.6 %copy.60 = bf16[56,768,256]{1,2,0:T(8,128)(2,1)} copy(bf16[56,768,256]{2,1,0:T(8,128)(2,1)} %bitcast.150) | data formatting | bytes 44040192 | tf_op jit(solution)/shard_map/jit(_take)/gather | solution.py:50
  486.9 23.6 %fusion.2 = f32[56,256,256]{1,2,0:T(8,128)} fusion(bf16[56,768,256]{1,2,0:T(8,128)(2,1)} %copy.60, pred[56,768]{1,0:T(8,128)(4,1)S(1)} %compare_and_fusion, pred[56,768]{1,0:T(8,128)(4,1)S(1)} %get-tuple-element.21), kind=kOutput, calls=%fused_computation.10 | convolution fusion | flops 5659164672 | bytes 36786176 | tf_op jit(solution)/shard_map/urk,url->ukl/dot_general | solution.py:53
  513.0 10.3 fusion.1
  523.3 11.1 fusion
  534.4 2.9 collective-permute-start
  538.0 106.1 %reduce-scatter.4.cloned.1.call-done = f32[14,256,256]{1,2,0:T(8,128)} async-done(((f32[56,256,256]{1,2,0:T(8,128)}), f32[14,256,256]{1,2,0:T(8,128)}) %reduce-scatter.4.cloned.1.call-update) | async-done | bytes 3670032 | tf_op jit(solution)/shard_map/reduce_scatter | solution.py:56
  644.2 4.2 multiply_add_fusion
  648.3 5.1 copy.63
  653.5 3.8 fusion.9
  659.1 164.1 %custom-call.20 = f32[14,128,128]{2,1,0:T(8,128)S(1)} custom-call(f32[14,128,128]{2,1,0:T(8,128)S(1)} %cholesky.122), custom_call_target="Cholesky" | custom-call | tf_op jit(solution)/shard_map/jit(cholesky)/cholesky | solution.py:18
  825.5 137.5 %custom-call.21 = f32[14,1,128,128]{2,3,1,0:T(8,128)S(1)} custom-call(f32[14,1,128,128]{3,2,1,0:T(8,128)S(1)} %select_bitcast_fusion), custom_call_target="InvertDiagBlocksLowerTriangular" | custom-call | tf_op jit(solution)/shard_map/jit(cholesky)/cholesky | solution.py:18
  963.1 3.2 constant_dynamic-update-slice_fusion.1
  966.2 3.2 convolution_subtract_fusion
  969.5 164.3 %custom-call.22 = f32[14,128,128]{2,1,0:T(8,128)S(1)} custom-call(f32[14,128,128]{2,1,0:T(8,128)S(1)} %convolution_subtract_fusion), custom_call_target="Cholesky" | custom-call | tf_op jit(solution)/shard_map/jit(cholesky)/cholesky | solution.py:18
  1135.0 4.4 select_select_fusion.3
  1139.5 8.9 while.1
  1140.1 4.0 bitcast_dynamic-update-slice_fusion.2
  1144.8 3.6 bitcast_dynamic-update-slice_fusion.2
  1148.4 276.1 %custom-call.23 = f32[14,2,128,128]{2,3,1,0:T(8,128)S(1)} custom-call(f32[14,2,128,128]{3,2,1,0:T(8,128)} %bitcast.163), custom_call_target="InvertDiagBlocksLowerTriangular" | custom-call | tf_op jit(solution)/shard_map/jit(_solve_triangular)/vmap()/triangular_solve | solution.py:14
  1425.4 2.7 fusion.19
  1435.1 9.0 all-gather
  1444.1 30.0 %bitcast_multiply_fusion = f32[43008,256]{1,0:T(8,128)} fusion(f32[56,256]{1,0:T(8,128)S(1)} %bitcast.154, f32[43008]{0:T(1024)S(1)} %convert_multiply_fusion), kind=kLoop, calls=%fused_computation.7 | loop fusion | flops 11010048 | bytes 44269568 | tf_op jit(solution)/shard_map/mul | solution.py:64
  1474.1 234.7 %scatter_custom_fusion = f32[12288,256]{1,0:T(8,128)} fusion(s32[43008]{0:T(1024)S(1)} %reshape.350, f32[43008,256]{1,0:T(8,128)} %bitcast_multiply_fusion, f32[]{:T(128)} %constant.174.clone.1), kind=kCustom, calls=%fused_computation.15 | custom fusion | flops 11010048 | bytes 12583424 | tf_op jit(solution)/shard_map/scatter-add | solution.py:65
  1708.8 10.7 all-to-all-start.2
  1719.7 151.3 %all-to-all-done.2 = f32[32,3,128,256]{3,2,1,0:T(8,128)} async-done(((f32[32,3,128,256]{3,2,1,0:T(8,128)}), f32[32,3,128,256]{3,2,1,0:T(8,128)}, u32[]{:S(2)}, u32[]{:S(2)}) %all-to-all-start.2) | async-done | bytes 12582944 | tf_op jit(solution)/shard_map/all_to_all | solution.py:71
  1873.5 28.4 %scatter_fusion = f32[32,128,256]{2,1,0:T(8,128)} fusion(f32[32,128,256]{2,1,0:T(8,128)} %broadcast_in_dim.65, s32[96]{0:T(128)S(1)} %fusion.45, f32[96,128,256]{2,1,0:T(8,128)} %bitcast.37), kind=kCustom, calls=%fused_computation.4 | custom fusion | flops 3145728 | bytes 37749120 | tf_op jit(solution)/shard_map/scatter-add | solution.py:77
  (94 shorter events, 24.5 us)
Async XLA Ops:
  7.2 12.7 copy-start
  8.7 23.2 %all-to-all-start = ((bf16[32,1,1]{2,1,0:T(2,128)(2,1)}), bf16[32,1,1]{2,1,0:T(2,128)(2,1)S(1)}, u32[]{:S(2)}, u32[]{:S(2)}) async-start(bf16[32,1,1]{2,1,0:T(2,128)(2,1)} %copy.57), calls=%async_computation | async-start | bytes 32768 | tf_op jit(solution)/shard_map/all_to_all | solution.py:41
  31.9 8.1 copy-start.3
  31.9 263.7 %all-to-all-start.1 = ((bf16[32,3,128,256]{3,2,1,0:T(8,128)(2,1)}), bf16[32,3,128,256]{3,2,1,0:T(8,128)(2,1)}, u32[]{:S(2)}, u32[]{:S(2)}) async-start(bf16[32,3,128,256]{3,2,1,0:T(8,128)(2,1)} %broadcast_select_fusion), calls=%async_computation.1 | async-start | bytes 12582912 | tf_op jit(solution)/shard_map/all_to_all | solution.py:40
  39.5 604.7 %reduce-scatter.4.cloned.1.call-start = ((), (), s32[]{:S(2)}) async-start(), calls=%async_computation.4 | async-start | bytes 18350080 | tf_op jit(solution)/shard_map/reduce_scatter | solution.py:56
  41.0 254.4 %copy-start.4 = (bf16[1,56,768]{2,1,0:T(8,128)(2,1)S(1)}, bf16[1,56,768]{2,1,0:T(8,128)(2,1)}, u32[]{:S(2)}) copy-start(bf16[1,56,768]{2,1,0:T(8,128)(2,1)} %param.12) | copy-start | bytes 258052
  510.6 0.9 copy-start.5
  510.6 1.1 copy-start.11
  513.0 25.0 %copy-start.10 = (f32[256]{0:T(256)S(1)}, f32[256]{0:T(256)}, u32[]{:S(2)}) copy-start(f32[256]{0:T(256)} %param.15) | copy-start | bytes 3076
  534.4 3.5 collective-permute-start
  538.0 110.3 %copy-start.7 = (f32[14,256,1]{1,0,2:T(8,128)}, f32[14,256,1]{1,0,2:T(8,128)S(1)}, u32[]{:S(2)}) copy-start(f32[14,256,1]{1,0,2:T(8,128)S(1)} %fusion.37) | copy-start | bytes 43012
  657.3 1.8 copy-start.2
  1139.5 285.0 %slice-start = ((f32[14,256,1]{1,0,2:T(8,128)}), f32[14,128,1]{1,0,2:T(8,128)S(1)}, s32[]{:S(2)}) async-start(f32[14,256,1]{1,0,2:T(8,128)} %copy-done.7), calls=%async_computation.5 | async-start | bytes 16384 | tf_op jit(solution)/shard_map/jit(_solve_triangular)/vmap()/triangular_solve | solution.py:14
  1139.5 288.6 %copy-start.8 = (f32[14,256,1]{1,0,2:T(8,128)S(1)}, f32[14,256,1]{1,0,2:T(8,128)}, u32[]{:S(2)}) copy-start(f32[14,256,1]{1,0,2:T(8,128)} %copy-done.7) | copy-start | bytes 43012
  1444.1 30.0 %copy-start.6 = (f32[56,256,1]{1,0,2:T(8,128)}, f32[56,256,1]{1,0,2:T(8,128)S(1)}, u32[]{:S(2)}) copy-start(f32[56,256,1]{1,0,2:T(8,128)S(1)} %copy.119) | copy-start | bytes 172036
  1708.8 10.7 copy-start.9
  1708.8 162.2 %all-to-all-start.2 = ((f32[32,3,128,256]{3,2,1,0:T(8,128)}), f32[32,3,128,256]{3,2,1,0:T(8,128)}, u32[]{:S(2)}, u32[]{:S(2)}) async-start(f32[32,3,128,256]{3,2,1,0:T(8,128)} %bitcast.152), calls=%async_computation.3 | async-start | bytes 25165824 | tf_op jit(solution)/shard_map/all_to_all | solution.py:71
  1873.5 28.4 %copy-start.1 = (bf16[1,32,128,256]{3,2,1,0:T(8,128)(2,1)S(1)}, bf16[1,32,128,256]{3,2,1,0:T(8,128)(2,1)}, u32[]{:S(2)}) copy-start(bf16[1,32,128,256]{3,2,1,0:T(8,128)(2,1)} %param.8) | copy-start | bytes 6291460
Sparse Core Ops, SparseCore 0:
  510.7 133.4 reduce-scatter.3
where the time goes:
time: 1920 us; the launch traced here: 1910 us
  other arithmetic  1060 us (55%)
  local copies, waits for them, and re-layouts  475 us (25%)
  waiting for transfers between devices  258 us (13%)
  matrix products  49.9 us (3%)
  starting transfers between devices  31.1 us (2%)
  blocking collectives  20.1 us (1%)
    another operation x9, other arithmetic, solve_users(): lower = jnp.linalg.cholesky(prior_prec[None] + ALPHA * gram)  467 us
    another operation x7, other arithmetic, tri_solve(): jax.scipy.linalg.solve_triangular(lower, right, lower=True, trans=transpose)  281 us
    gather x2, local copies, waits for them, and re-layouts, on_device(): live = column < arrived_counts[source]  254 us
    scatter-add x1, other arithmetic, on_device(): jax.ops.segment_sum(terms.reshape(-1, rank), refs.reshape(-1), num_segmen...  235 us
    gather x2, local copies, waits for them, and re-layouts, on_device(): rows = jnp.take(flat_rows, refs, axis=0)  191 us
    all_to_all x1, waiting for transfers between devices, on_device(): lax.all_to_all(contrib, 'usr', split_axis=0, concat_axis=0, tiled=True)  151 us
    reduce_scatter x1, waiting for transfers between devices, on_device(): lax.psum_scatter(gram, 'grp', scatter_dimension=0, tiled=True)  106 us
  transfers between devices with their start and end apart: 5, of which 3 were waited for; matrix products, arithmetic and copies ran while one was open for 15% of the time, Pallas kernels for 0%

commit v1 on v0

v1 whole, which is shorter than its diff:
```python
import functools

import jax
import jax.numpy as jnp
from jax import lax
from jax.experimental import pallas as pl
from jax.experimental.pallas import tpu as pltpu
from jax.sharding import PartitionSpec as P

ALPHA = 2.0
F32 = jnp.float32
BF16 = jnp.bfloat16
MIB = 2**20


def iota(shape, dim):
    return lax.broadcasted_iota(jnp.int32, shape, dim)


def split(x):
    hi = x.astype(BF16).astype(F32)
    return hi, x - hi


def stacked(x):
    hi, lo = split(x)
    left = jnp.concatenate([hi, hi, lo, lo], axis=0).astype(BF16)
    right = jnp.concatenate([hi, lo, hi, lo], axis=0).astype(BF16)
    return left, right


def dot_tn(a, b):
    return lax.dot_general(a, b, (((0,), (0,)), ((), ())), preferred_element_type=F32)


def pick_kernel(cols, per_step, listed, live, blocks, out):
    base = pl.program_id(0) * per_step

    def body(i, carry):
        keep = live[base + i] > 0
        block = blocks[listed[base + i]]
        out[i] = jnp.where(keep, block, jnp.zeros_like(block))
        return carry

    lax.fori_loop(0, per_step, body, 0)


def pick_blocks(blocks, listed, live):
    n = listed.shape[0]
    owned, height, rank = blocks.shape
    steps = 4
    per_step = n // steps
    return pl.pallas_call(
        functools.partial(pick_kernel, n, per_step),
        grid_spec=pltpu.PrefetchScalarGridSpec(
            num_scalar_prefetch=2,
            grid=(steps,),
            in_specs=[pl.BlockSpec((owned, height, rank), lambda s, *_: (0, 0, 0))],
            out_specs=pl.BlockSpec((per_step, height, rank), lambda s, *_: (s, 0, 0)),
        ),
        out_shape=jax.ShapeDtypeStruct((n, height, rank), BF16),
        compiler_params=pltpu.CompilerParams(vmem_limit_bytes=32 * MIB),
        name="pick_blocks",
    )(listed, live, blocks)


def weight_kernel(refs, values, out):
    n_blocks, users, height = out.shape
    slots = refs.shape[1]
    for u in range(users):
        ref = refs[u : u + 1, :]
        value = values[u : u + 1, :].astype(F32)
        block = ref // height
        row = ref % height
        hot_block = jnp.where(iota((n_blocks, slots), 0) == block, value, 0.0).astype(BF16)
        hot_row = jnp.where(iota((height, slots), 0) == row, 1.0, 0.0).astype(BF16)
        out[:, u, :] = lax.dot_general(hot_block, hot_row, (((1,), (1,)), ((), ())), preferred_element_type=F32)


def make_weights(refs, values, n_blocks, height):
    users, slots = refs.shape
    group = 8
    return pl.pallas_call(
        weight_kernel,
        grid=(users // group,),
        in_specs=[pl.BlockSpec((group, slots), lambda i: (i, 0))] * 2,
        out_specs=pl.BlockSpec((n_blocks, group, height), lambda i: (0, i, 0)),
        out_shape=jax.ShapeDtypeStruct((n_blocks, users, height), F32),
        compiler_params=pltpu.CompilerParams(vmem_limit_bytes=32 * MIB),
        name="make_weights",
    )(refs, values)


def gram_kernel(refs, table, values, out, wide, picked):
    rows = table.shape[0]
    slots = refs.shape[2]
    chunk, unroll = 128, 32

    @pl.when(pl.program_id(0) == 0)
    def _():
        def widen(i, carry):
            part = table[pl.ds(i * chunk, chunk), :].astype(F32)
            wide[pl.ds(i * 2 * chunk, chunk, stride=2), :] = part[:, :128]
            wide[pl.ds(i * 2 * chunk + 1, chunk, stride=2), :] = part[:, 128:]
            return carry

        lax.fori_loop(0, rows // chunk, widen, 0)

    def fetch(i, carry):
        base = i * unroll
        got = [wide[pl.ds(pl.multiple_of(refs[0, 0, base + j] * 2, 2), 2), :] for j in range(unroll)]
        for j in range(unroll):
            picked[pl.ds(pl.multiple_of((base + j) * 2, 2), 2), :] = got[j]
        return carry

    lax.fori_loop(0, slots // unroll, fetch, 0)
    low = picked[pl.ds(0, slots, stride=2), :].astype(BF16)
    high = picked[pl.ds(1, slots, stride=2), :].astype(BF16)
    mat = jnp.concatenate([low, high], axis=1)
    gram = dot_tn(mat, mat)
    linear = lax.dot_general(
        jnp.broadcast_to(values[0], (8, slots)), mat, (((1,), (0,)), ((), ())), preferred_element_type=F32
    )
    r, c = iota((128, 128), 0), iota((128, 128), 1)
    last = gram[128:, 128:]
    out[0, :128, :] = jnp.where(r >= c, gram[:128, :128], last)
    out[0, 128:256, :] = gram[:128, 128:]
    diag = jnp.sum(jnp.where(r == c, last, 0.0), axis=0, keepdims=True)
    row = iota((8, 128), 0)
    tail = jnp.where(row == 1, linear[:, :128], jnp.where(row == 2, linear[:, 128:], 0.0))
    out[0, 256:264, :] = jnp.where(row == 0, diag, tail)


def gram_terms(table, refs, values):
    users, slots = refs.shape
    rows, rank = table.shape
    return pl.pallas_call(
        gram_kernel,
        grid=(users,),
        in_specs=[
            pl.BlockSpec((1, 1, slots), lambda u: (u, 0, 0), memory_space=pltpu.SMEM),
            pl.BlockSpec((rows, rank), lambda u: (0, 0), pipeline_mode=pl.Buffered(1)),
            pl.BlockSpec((1, 1, slots), lambda u: (u, 0, 0)),
        ],
        out_specs=pl.BlockSpec((1, 264, 128), lambda u: (u, 0, 0)),
        out_shape=jax.ShapeDtypeStruct((users, 264, 128), F32),
        scratch_shapes=[pltpu.VMEM((2 * rows, 128), F32), pltpu.VMEM((2 * slots, 128), F32)],
        compiler_params=pltpu.CompilerParams(vmem_limit_bytes=48 * MIB),
        name="gram_terms",
    )(refs.reshape(users, 1, slots), table, values.reshape(users, 1, slots))


def solve_kernel(packed, noise_cols, prior, shift, out, mats, right, back, sums):
    users = packed.shape[0]
    rank = prior.shape[0]
    half = rank // 2
    step, outer = 8, 64

    r, c = iota((half, half), 0), iota((half, half), 1)
    for m in range(users):
        both = packed[m, :half, :]
        cross = packed[m, half:rank, :]
        turned = both.T
        diag = packed[m, rank : rank + 1, :]
        first = jnp.where(r >= c, both, turned)
        last = jnp.where(r < c, both, jnp.where(r == c, diag, turned))
        mats[m, :half, :half] = prior[:half, :half] + ALPHA * first
        mats[m, :half, half:] = prior[:half, half:] + ALPHA * cross
        mats[m, half:, half:] = prior[half:, half:] + ALPHA * last
        mats[m, half:, :half] = jnp.zeros((half, half), F32)
        right[m, 0:1, :half] = ALPHA * packed[m, rank + 1 : rank + 2, :] + shift[:, :half]
        right[m, 0:1, half:] = ALPHA * packed[m, rank + 2 : rank + 3, :] + shift[:, half:]

    sub = iota((1, step, 128), 1)
    lane = iota((1, step, 128), 2)
    wide_lane = iota((step, rank), 1)
    unit = jnp.where(lane == sub + step, 1.0, 0.0)

    for o in range(rank // outer):
        lo = o * outer

        def panel(i, carry, lo=lo):
            k0 = pl.multiple_of(lo + i * step, step)
            rows = mats[:, pl.ds(k0, step), :]
            turn = (rank - k0) % rank
            aux = jnp.stack([pltpu.roll(rows[m], turn, 1)[:, :128] for m in range(users)])
            aux = jnp.where(lane < step, aux, unit)
            for k in range(step):
                col = aux[:, :, k : k + 1]
                factor = jnp.where(sub[:, :, :1] > k, col / col[:, k : k + 1, :], 0.0)
                aux = aux - factor * aux[:, k : k + 1, :]
                rows = rows - factor * rows[:, k : k + 1, :]
            pivots = jnp.sum(jnp.where(lane == sub, aux, 0.0), axis=2, keepdims=True)
            scale = lax.rsqrt(pivots)
            rows = rows * scale
            inverse = jnp.where((lane >= step) & (lane < 2 * step), aux * scale, 0.0)
            mats[:, pl.ds(k0, step), :] = rows
            noise = noise_cols[pl.ds(k0, step), :]
            for m in range(users):
                spread = jnp.concatenate([inverse[m], jnp.zeros((step, rank - 128), F32)], axis=1)
                spread = pltpu.roll(spread, (k0 + rank - step) % rank, 1)
                back[m, pl.ds(k0, step), :] = spread
                given = right[m, 0:1, :]
                y = jnp.sum(spread * given, axis=1, keepdims=True)
                right[m, 0:1, :] = given - jnp.sum(y * rows[m], axis=0, keepdims=True)
                sums[m, pl.ds(k0, step), :] = jnp.broadcast_to(y + noise[:, m : m + 1], (step, 128))
                hi, rest = split(rows[m])
                later = wide_lane >= k0 + step
                left = jnp.concatenate([hi, hi, rest, rest], axis=0)
                left = jnp.where(jnp.concatenate([later] * 4, axis=0), left, 0.0)[:, lo : lo + outer].astype(BF16)
                other = jnp.concatenate([hi, rest, hi, rest], axis=0).astype(BF16)
                mats[m, lo : lo + outer, :] = mats[m, lo : lo + outer, :] - dot_tn(left, other)
            return carry

        lax.fori_loop(0, outer // step, panel, 0)
        if lo + outer < rank:
            start = (lo + outer) // 128 * 128

            def trail(m, carry, lo=lo, start=start):
                left, other = stacked(mats[m, lo : lo + outer, :])
                mats[m, lo + outer :, start:] = mats[m, lo + outer :, start:] - dot_tn(
                    left[:, lo + outer :], other[:, start:]
                )
                return carry

            lax.fori_loop(0, users, trail, 0)

    def backward(i, x):
        k0 = pl.multiple_of(rank - step - i * step, step)
        rows = mats[:, pl.ds(k0, step), :]
        rest = sums[:, pl.ds(k0, step), :][:, :, :1] - jnp.sum(rows * x, axis=2, keepdims=True)
        return x + jnp.sum(back[:, pl.ds(k0, step), :] * rest, axis=1, keepdims=True)

    x = lax.fori_loop(0, rank // step, backward, jnp.zeros((users, 1, rank), F32))
    for m in range(users):
        out[m : m + 1, :] = x[m]


def solve_users(packed, noise, prior, shift):
    users = packed.shape[0]
    rank = prior.shape[0]
    vmem = pl.BlockSpec(memory_space=pltpu.VMEM)
    return pl.pallas_call(
        solve_kernel,
        in_specs=[vmem] * 4,
        out_specs=vmem,
        out_shape=jax.ShapeDtypeStruct((users, rank), F32),
        scratch_shapes=[
            pltpu.VMEM((users, rank, rank), F32),
            pltpu.VMEM((users, 8, rank), F32),
            pltpu.VMEM((users, rank, rank), F32),
            pltpu.VMEM((users, rank, 128), F32),
        ],
        compiler_params=pltpu.CompilerParams(vmem_limit_bytes=48 * MIB),
        name="solve_users",
    )(packed, noise.T, prior, shift.reshape(1, rank))


def stats_kernel(cols, listed, live, weights, samples, out):
    out[...] = jnp.zeros_like(out)

    def device(d, carry):
        hi, lo = split(samples[d])
        other = jnp.concatenate([hi, lo, hi, lo], axis=0).astype(BF16)
        for c in range(cols):
            i = d * cols + c
            own = jnp.where(live[i] > 0, ALPHA * weights[i], 0.0)
            hi, lo = split(own)
            left = jnp.concatenate([hi, hi, lo, lo], axis=0).astype(BF16)
            b = listed[i]
            out[b] = out[b] + dot_tn(left, other)
        return carry

    lax.fori_loop(0, samples.shape[0], device, 0)


def make_stats(weights, samples, listed, live, owned):
    n, users, height = weights.shape
    peers, _, rank = samples.shape
    vmem = pl.BlockSpec(memory_space=pltpu.VMEM)
    smem = pl.BlockSpec(memory_space=pltpu.SMEM)
    return pl.pallas_call(
        functools.partial(stats_kernel, n // peers),
        in_specs=[smem, smem, vmem, vmem],
        out_specs=vmem,
        out_shape=jax.ShapeDtypeStruct((owned, height, rank), F32),
        compiler_params=pltpu.CompilerParams(vmem_limit_bytes=32 * MIB),
        name="make_stats",
    )(listed, live, weights, samples)


def on_device(item_factors, send_ids, send_count, rating_pointer, rating_value, noise, prior_prec, prior_shift):
    peers = lax.axis_size("usr")
    blocks = item_factors[0]
    owned, height, rank = blocks.shape
    cols = send_ids.shape[-1]
    n = peers * cols
    listed = send_ids[0, 0].reshape(n)
    live = (jnp.arange(cols, dtype=jnp.int32)[None, :] < send_count[0, 0][:, None]).astype(jnp.int32).reshape(n)
    refs, values = rating_pointer[0], rating_value[0]

    outgoing = pick_blocks(blocks, listed, live)
    incoming = lax.all_to_all(outgoing, "usr", split_axis=0, concat_axis=0, tiled=True)
    weights = make_weights(refs, values, n, height)
    gathered = lax.all_to_all(weights, "usr", split_axis=0, concat_axis=0, tiled=True)

    packed = gram_terms(incoming.reshape(n * height, rank), refs, values)
    packed = lax.psum_scatter(packed, "grp", scatter_dimension=0, tiled=True)
    share = packed.shape[0]
    draws = lax.dynamic_slice_in_dim(noise, lax.axis_index("grp") * share, share, 0)
    own = solve_users(packed, draws, prior_prec, prior_shift)
    everyone = lax.all_gather(own, ("usr", "grp"), axis=0, tiled=True).reshape(peers, refs.shape[0], rank)
    samples = lax.dynamic_index_in_dim(everyone, lax.axis_index("usr"), 0, keepdims=False)
    stats = make_stats(gathered, everyone, listed, live, owned)
    return (samples, stats[None])


def solution(mesh):
    placed = (
        P("grp", "usr", None, None),
        P("grp", "usr", None, None),
        P("grp", "usr", None),
        P("grp", "usr", None),
        P("grp", "usr", None),
        P("usr", None),
        P(),
        P(),
    )
    return jax.shard_map(
        on_device,
        mesh=mesh,
        in_specs=placed,
        out_specs=(P("usr", None), P("grp", "usr", None, None)),
        check_vma=False,
    )
```

time: 1920 us -> 412 us (0.21)
  other arithmetic: 1060 us -> 0.73 us
  local copies, waits for them, and re-layouts: 475 us -> 14.2 us
  Pallas kernels: 0 us -> 153 us
  matrix products: 49.9 us -> 0 us
  waiting for transfers between devices: 258 us -> 212 us
  blocking collectives: 20.1 us -> 0 us
    another operation x16 -> x0, other arithmetic: 748 us -> none  [the longest x9 467 us: solve_users(): lower = jnp.linalg.cholesky(prior_prec[None] + ALPHA * gram)]
    gather x5 -> x0, local copies, waits for them, and re-layouts: 452 us -> none  [the longest x2 254 us: on_device(): live = column < arrived_counts[source]]
    scatter-add x2 -> x0, other arithmetic: 263 us -> none  [the longest x1 235 us: on_device(): jax.ops.segment_sum(terms.reshape(-1, rank), refs.reshape(-1), num_segmen...]
    pallas_call x0 -> x5, Pallas kernels: none -> 153 us  [the longest x1 76.1 us: gram_terms(): pl.pallas_call(gram_kernel, grid=(users,), in_specs=[pl.BlockSpec((1, 1,...]
    all_to_all x2 -> x1, waiting for transfers between devices: 151 us -> 0.01 us  [on_device(): lax.all_to_all(weights, 'usr', split_axis=0, concat_axis=0, tiled=True)]
    all_to_all x1, waiting for transfers between devices: 0.01 us -> 72.6 us  [on_device(): lax.all_to_all(outgoing, 'usr', split_axis=0, concat_axis=0, tiled=True)]
    all_gather x0 -> x1, waiting for transfers between devices: none -> 63.5 us  [on_device(): lax.all_gather(own, ('usr', 'grp'), axis=0, tiled=True)]
    dot_general x2 -> x0, matrix products: 33.9 us -> none  [the longest x1 23.6 us: on_device(): jnp.einsum('urk,url->ukl', masked, masked, preferred_element_type=jnp.flo...]
  transfers between devices with their start and end apart: 5 -> 4, of which waited for: 3 -> 3; matrix products, arithmetic and copies ran while one was open for 15% -> 1% of each run, Pallas kernels for 0% -> 1%
where the time goes in v1:
time: 412 us; the launch traced here: 411 us
  waiting for transfers between devices  212 us (51%)
  Pallas kernels  153 us (37%)
  starting transfers between devices  17.3 us (4%)
  local copies, waits for them, and re-layouts  14.2 us (3%)
  between operations  14.2 us (3%)
    pallas_call x1, Pallas kernels, gram_terms(): pl.pallas_call(gram_kernel, grid=(users,), in_specs=[pl.BlockSpec((1, 1,...  76.1 us
    reduce_scatter x1, waiting for transfers between devices, on_device(): packed = lax.psum_scatter(packed, 'grp', scatter_dimension=0, tiled=True)  76 us
    all_to_all x1, waiting for transfers between devices, on_device(): lax.all_to_all(outgoing, 'usr', split_axis=0, concat_axis=0, tiled=True)  72.6 us
    all_gather x1, waiting for transfers between devices, on_device(): lax.all_gather(own, ('usr', 'grp'), axis=0, tiled=True)  63.5 us
    pallas_call x1, Pallas kernels, solve_users(): pl.pallas_call(solve_kernel, in_specs=[vmem] * 4, out_specs=vmem, out_sha...  57.1 us
    pallas_call x1, Pallas kernels, make_stats(): pl.pallas_call(functools.partial(stats_kernel, n // peers), in_specs=[sme...  11.6 us
    unnamed x22, local copies, waits for them, and re-layouts  9.71 us
    all_to_all x1, starting transfers between devices, on_device(): lax.all_to_all(outgoing, 'usr', split_axis=0, concat_axis=0, tiled=True)  9.61 us
  transfers between devices with their start and end apart: 4, of which 3 were waited for; matrix products, arithmetic and copies ran while one was open for 1% of the time, Pallas kernels for 1%

profile of v1, /device:TPU:1, one launch (start us, length us, event | category | flops | bytes accessed | tf_op | source)
XLA Modules:
  0.0 411.3 jit_solution(937860695873388892)
XLA Ops:
  7.2 0.0 copy-start
  7.2 0.8 copy.15
  8.0 0.1 reshape_squeeze.10.listed
  8.1 0.7 fusion
  8.8 0.1 reshape.23.live
  8.9 0.0 copy-start.4
  8.9 1.6 copy-done.4
  10.5 2.0 pick_blocks.1
  12.5 2.7 copy-done.1
  15.1 9.6 %all-to-all-start = ((bf16[96,128,256]{2,1,0:T(8,128)(2,1)}), bf16[96,128,256]{2,1,0:T(8,128)(2,1)}, u32[]{:S(2)}, u32[]{:S(2)}) async-start(bf16[96,128,256]{2,1,0:T(8,128)(2,1)} %copy-done.1), calls=%async_computation | async-start | bytes 12582912 | tf_op jit(solution)/shard_map/all_to_all | solution.py:303
  24.8 0.0 reduce-scatter.2.cloned.1.call-start
  24.8 0.1 reshape_squeeze.9.refs
  25.0 0.1 copy.16.values
  25.1 72.6 %all-to-all-done = bf16[96,128,256]{2,1,0:T(8,128)(2,1)} async-done(((bf16[96,128,256]{2,1,0:T(8,128)(2,1)}), bf16[96,128,256]{2,1,0:T(8,128)(2,1)}, u32[]{:S(2)}, u32[]{:S(2)}) %all-to-all-start) | async-done | bytes 6291488 | tf_op jit(solution)/shard_map/all_to_all | solution.py:303
  97.7 76.1 %gram_terms.1 = f32[56,264,128]{2,1,0:T(8,128)} custom-call(s32[56,1,768]{2,1,0:T(1,128)S(1)} %reshape_squeeze.9.refs, bf16[12288,256]{1,0:T(8,128)(2,1)} %bitcast.2.table, bf16[56,1,768]{2,1,0:T(2,128)(2,1)S(1)} %copy.16.values), custom_call_target="tpu_custom_call" | custom-call | tf_op jit(solution)/shard_map/gram_terms/pallas_call | solution.py:137
  173.8 0.0 reduce-scatter.2.cloned.1.call-update
  173.8 0.0 all-gather.3.cloned.1.call-start
  173.9 0.1 copy.18
  174.0 76.0 %reduce-scatter.2.cloned.1.call-done.packed = f32[14,264,128]{2,1,0:T(8,128)} async-done(((f32[56,264,128]{2,1,0:T(8,128)}), f32[14,264,128]{2,1,0:T(8,128)}) %reduce-scatter.2.cloned.1.call-update) | async-done | bytes 1892368 | tf_op jit(solution)/shard_map/reduce_scatter | solution.py:308
  250.0 1.5 copy-done.5
  251.5 57.1 %solve_users.1 = f32[14,256]{1,0:T(8,128)} custom-call(f32[14,264,128]{2,1,0:T(8,128)S(1)} %copy-done.5, f32[256,14]{1,0:T(8,128)S(1)} %bitcast.16, f32[256,256]{1,0:T(8,128)S(1)} %copy-done.8, f32[1,256]{1,0:T(1,128)S(1)} %bitcast.19), custom_call_target="tpu_custom_call" | custom-call | tf_op jit(solution)/shard_map/solve_users/pallas_call | solution.py:243
  308.6 0.0 all-gather.3.cloned.1.call-update
  308.6 6.1 %make_weights.1 = f32[96,56,128]{2,1,0:T(8,128)S(1)} custom-call(s32[56,768]{1,0:T(8,128)S(1)} %bitcast.15, bf16[56,768]{1,0:T(8,128)(2,1)S(1)} %bitcast.18), custom_call_target="tpu_custom_call" | custom-call | tf_op jit(solution)/shard_map/make_weights/pallas_call | solution.py:83
  314.7 0.0 copy-start.2
  314.7 1.5 copy-done.2
  316.3 7.6 %all-to-all-start.1 = ((f32[96,56,128]{2,1,0:T(8,128)}), f32[96,56,128]{2,1,0:T(8,128)S(1)}, u32[]{:S(2)}, u32[]{:S(2)}) async-start(f32[96,56,128]{2,1,0:T(8,128)} %copy-done.2), calls=%async_computation.2 | async-start | bytes 5505024 | tf_op jit(solution)/shard_map/all_to_all | solution.py:305
  323.9 63.5 %all-gather.3.cloned.1.call-done = f32[128,14,256]{2,1,0:T(8,128)} async-done(((f32[1,14,256]{2,1,0:T(8,128)}), f32[128,14,256]{2,1,0:T(8,128)}) %all-gather.3.cloned.1.call-update) | async-done | bytes 1835024 | tf_op jit(solution)/shard_map/all_gather | solution.py:312
  387.4 2.6 reshape.22.samples
  390.0 1.4 dynamic-slice_bitcast_fusion
  391.4 0.0 all-to-all-done.1.weights
  391.4 1.5 copy-done.3
  392.9 11.6 %make_stats.1 = f32[32,128,256]{2,1,0:T(8,128)} custom-call(s32[96]{0:T(128)S(1)} %reshape_squeeze.10.listed, s32[96]{0:T(128)S(1)} %reshape.23.live, f32[96,56,128]{2,1,0:T(8,128)S(1)} %all-to-all-done.1.weights, f32[32,56,256]{2,1,0:T(8,128)S(1)} %copy-done.3), custom_call_target="tpu_custom_call" | custom-call | tf_op jit(solution)/shard_map/make_stats/pallas_call | solution.py:282
  (13 shorter events, 0.0 us)
Async XLA Ops:
  7.2 166.7 %copy-start = (f32[56,256]{1,0:T(8,128)S(1)}, f32[56,256]{1,0:T(8,128)}, u32[]{:S(2)}) copy-start(f32[56,256]{1,0:T(8,128)} %param.13) | copy-start | bytes 172036
  8.9 1.6 copy-start.4
  12.5 2.7 copy-start.1
  15.1 9.7 %copy-start.6 = (s32[1,56,768]{2,1,0:T(8,128)S(1)}, s32[1,56,768]{2,1,0:T(8,128)}, u32[]{:S(2)}) copy-start(s32[1,56,768]{2,1,0:T(8,128)} %param.11) | copy-start | bytes 516100
  15.1 9.8 %copy-start.7 = (bf16[1,56,768]{2,1,0:T(8,128)(2,1)S(1)}, bf16[1,56,768]{2,1,0:T(8,128)(2,1)}, u32[]{:S(2)}) copy-start(bf16[1,56,768]{2,1,0:T(8,128)(2,1)} %param.12) | copy-start | bytes 258052
  15.1 82.6 %all-to-all-start = ((bf16[96,128,256]{2,1,0:T(8,128)(2,1)}), bf16[96,128,256]{2,1,0:T(8,128)(2,1)}, u32[]{:S(2)}, u32[]{:S(2)}) async-start(bf16[96,128,256]{2,1,0:T(8,128)(2,1)} %copy-done.1), calls=%async_computation | async-start | bytes 12582912 | tf_op jit(solution)/shard_map/all_to_all | solution.py:303
  24.8 225.2 %reduce-scatter.2.cloned.1.call-start = ((), (), s32[]{:S(2)}) async-start(), calls=%async_computation.3 | async-start | bytes 9461760 | tf_op jit(solution)/shard_map/reduce_scatter | solution.py:308
  173.8 76.2 %copy-start.8 = (f32[256,256]{1,0:T(8,128)S(1)}, f32[256,256]{1,0:T(8,128)}, u32[]{:S(2)}) copy-start(f32[256,256]{1,0:T(8,128)} %prior.1) | copy-start | bytes 786436
  173.8 76.2 %copy-start.9 = (f32[256]{0:T(256)S(1)}, f32[256]{0:T(256)}, u32[]{:S(2)}) copy-start(f32[256]{0:T(256)} %param.15) | copy-start | bytes 3076
  173.8 213.5 %all-gather.3.cloned.1.call-start = ((), (), s32[]{:S(2)}) async-start(), calls=%async_computation.4 | async-start | bytes 2113536 | tf_op jit(solution)/shard_map/all_gather | solution.py:312
  250.0 1.5 copy-start.5
  314.7 1.5 copy-start.2
  316.3 75.2 %all-to-all-start.1 = ((f32[96,56,128]{2,1,0:T(8,128)}), f32[96,56,128]{2,1,0:T(8,128)S(1)}, u32[]{:S(2)}, u32[]{:S(2)}) async-start(f32[96,56,128]{2,1,0:T(8,128)} %copy-done.2), calls=%async_computation.2 | async-start | bytes 5505024 | tf_op jit(solution)/shard_map/all_to_all | solution.py:305
  391.4 1.5 copy-start.3
Sparse Core Ops, SparseCore 0:
  173.9 76.0 reduce-scatter.1
  308.7 78.5 all-gather.2

commit v2 on v1

--- a/solution.py
+++ b/solution.py
@@ -91,63 +91,78 @@
     )(refs, values)
 
 
-def gram_kernel(refs, table, values, out, wide, picked):
-    rows = table.shape[0]
-    slots = refs.shape[2]
-    chunk, unroll = 128, 32
-
-    @pl.when(pl.program_id(0) == 0)
-    def _():
-        def widen(i, carry):
-            part = table[pl.ds(i * chunk, chunk), :].astype(F32)
-            wide[pl.ds(i * 2 * chunk, chunk, stride=2), :] = part[:, :128]
-            wide[pl.ds(i * 2 * chunk + 1, chunk, stride=2), :] = part[:, 128:]
-            return carry
-
-        lax.fori_loop(0, rows // chunk, widen, 0)
-
-    def fetch(i, carry):
-        base = i * unroll
-        got = [wide[pl.ds(pl.multiple_of(refs[0, 0, base + j] * 2, 2), 2), :] for j in range(unroll)]
+def gather_rows(wide, picked, refs, user):
+    slots = picked.shape[0] // 2
+    unroll = 16
+    for base in range(0, slots, unroll):
+        got = [wide[pl.ds(pl.multiple_of(refs[user * slots + base + j], 2), 2), :] for j in range(unroll)]
         for j in range(unroll):
-            picked[pl.ds(pl.multiple_of((base + j) * 2, 2), 2), :] = got[j]
-        return carry
-
-    lax.fori_loop(0, slots // unroll, fetch, 0)
+            picked[2 * (base + j) : 2 * (base + j) + 2, :] = got[j]
+
+
+def packed_terms(picked, value, store):
+    slots = picked.shape[0] // 2
     low = picked[pl.ds(0, slots, stride=2), :].astype(BF16)
     high = picked[pl.ds(1, slots, stride=2), :].astype(BF16)
     mat = jnp.concatenate([low, high], axis=1)
     gram = dot_tn(mat, mat)
     linear = lax.dot_general(
-        jnp.broadcast_to(values[0], (8, slots)), mat, (((1,), (0,)), ((), ())), preferred_element_type=F32
+        jnp.broadcast_to(value, (8, slots)), mat, (((1,), (0,)), ((), ())), preferred_element_type=F32
     )
     r, c = iota((128, 128), 0), iota((128, 128), 1)
     last = gram[128:, 128:]
-    out[0, :128, :] = jnp.where(r >= c, gram[:128, :128], last)
-    out[0, 128:256, :] = gram[:128, 128:]
+    store(0, jnp.where(r >= c, gram[:128, :128], last))
+    store(128, gram[:128, 128:])
     diag = jnp.sum(jnp.where(r == c, last, 0.0), axis=0, keepdims=True)
     row = iota((8, 128), 0)
     tail = jnp.where(row == 1, linear[:, :128], jnp.where(row == 2, linear[:, 128:], 0.0))
-    out[0, 256:264, :] = jnp.where(row == 0, diag, tail)
+    store(256, jnp.where(row == 0, diag, tail))
+
+
+def gram_kernel(refs, table, values, out, wide, even, odd):
+    rows = table.shape[0]
+    users = out.shape[0]
+    chunk = 128
+
+    def widen(i, carry):
+        part = table[pl.ds(i * chunk, chunk), :].astype(F32)
+        wide[pl.ds(i * 2 * chunk, chunk, stride=2), :] = part[:, :128]
+        wide[pl.ds(i * 2 * chunk + 1, chunk, stride=2), :] = part[:, 128:]
+        return carry
+
+    lax.fori_loop(0, rows // chunk, widen, 0)
+
+    def terms(picked, u):
+        def store(at, part):
+            out[u, at : at + part.shape[0], :] = part
+
+        packed_terms(picked, values[pl.ds(u, 1), :].astype(BF16), store)
+
+    gather_rows(wide, even, refs, 0)
+
+    def pair(i, carry):
+        gather_rows(wide, odd, refs, 2 * i + 1)
+        terms(even, 2 * i)
+        gather_rows(wide, even, refs, lax.min(2 * i + 2, users - 1))
+        terms(odd, 2 * i + 1)
+        return carry
+
+    lax.fori_loop(0, users // 2, pair, 0)
 
 
 def gram_terms(table, refs, values):
     users, slots = refs.shape
     rows, rank = table.shape
+    vmem = pl.BlockSpec(memory_space=pltpu.VMEM)
     return pl.pallas_call(
         gram_kernel,
-        grid=(users,),
-        in_specs=[
-            pl.BlockSpec((1, 1, slots), lambda u: (u, 0, 0), memory_space=pltpu.SMEM),
-            pl.BlockSpec((rows, rank), lambda u: (0, 0), pipeline_mode=pl.Buffered(1)),
-            pl.BlockSpec((1, 1, slots), lambda u: (u, 0, 0)),
-        ],
-        out_specs=pl.BlockSpec((1, 264, 128), lambda u: (u, 0, 0)),
+        in_specs=[pl.BlockSpec(memory_space=pltpu.SMEM), vmem, vmem],
+        out_specs=vmem,
         out_shape=jax.ShapeDtypeStruct((users, 264, 128), F32),
-        scratch_shapes=[pltpu.VMEM((2 * rows, 128), F32), pltpu.VMEM((2 * slots, 128), F32)],
+        scratch_shapes=[pltpu.VMEM((2 * rows, 128), F32)] + [pltpu.VMEM((2 * slots, 128), F32)] * 2,
         compiler_params=pltpu.CompilerParams(vmem_limit_bytes=48 * MIB),
         name="gram_terms",
-    )(refs.reshape(users, 1, slots), table, values.reshape(users, 1, slots))
+    )((2 * refs).reshape(users * slots), table, values.astype(F32))
 
 
 def solve_kernel(packed, noise_cols, prior, shift, out, mats, right, back, sums):
@@ -302,10 +317,12 @@
     outgoing = pick_blocks(blocks, listed, live)
     incoming = lax.all_to_all(outgoing, "usr", split_axis=0, concat_axis=0, tiled=True)
     weights = make_weights(refs, values, n, height)
+    incoming, weights = lax.optimization_barrier((incoming, weights))
     gathered = lax.all_to_all(weights, "usr", split_axis=0, concat_axis=0, tiled=True)
 
     packed = gram_terms(incoming.reshape(n * height, rank), refs, values)
     packed = lax.psum_scatter(packed, "grp", scatter_dimension=0, tiled=True)
+    packed, gathered = lax.optimization_barrier((packed, gathered))
     share = packed.shape[0]
     draws = lax.dynamic_slice_in_dim(noise, lax.axis_index("grp") * share, share, 0)
     own = solve_users(packed, draws, prior_prec, prior_shift)

time: 412 us -> 376 us (0.913)
  Pallas kernels: 153 us -> 130 us
  waiting for transfers between devices: 212 us -> 198 us
    reduce_scatter x1, waiting for transfers between devices: 76 us -> 32 us  [on_device(): packed = lax.psum_scatter(packed, 'grp', scatter_dimension=0, tiled=True)]
    all_to_all x1, waiting for transfers between devices: 0.01 us -> 34.8 us  [on_device(): lax.all_to_all(weights, 'usr', split_axis=0, concat_axis=0, tiled=True)]
    pallas_call x1, Pallas kernels: 76.1 us -> 53.1 us  [gram_terms(): pl.pallas_call(gram_kernel, in_specs=[pl.BlockSpec(memory_space=pltpu.SME...]
    all_to_all x1, waiting for transfers between devices: 72.6 us -> 65.2 us  [on_device(): lax.all_to_all(outgoing, 'usr', split_axis=0, concat_axis=0, tiled=True)]
  transfers between devices with their start and end apart: 4 -> 4, of which waited for: 3 -> 4; matrix products, arithmetic and copies ran while one was open for 1% -> 0% of each run, Pallas kernels for 1% -> 2%
where the time goes in v2:
time: 376 us; the launch traced here: 375 us
  waiting for transfers between devices  198 us (53%)
  Pallas kernels  130 us (35%)
  starting transfers between devices  18.8 us (5%)
  between operations  14.2 us (4%)
  local copies, waits for them, and re-layouts  14 us (4%)
    all_gather x1, waiting for transfers between devices, on_device(): lax.all_gather(own, ('usr', 'grp'), axis=0, tiled=True)  65.5 us
    all_to_all x1, waiting for transfers between devices, on_device(): lax.all_to_all(outgoing, 'usr', split_axis=0, concat_axis=0, tiled=True)  65.2 us
    pallas_call x1, Pallas kernels, solve_users(): pl.pallas_call(solve_kernel, in_specs=[vmem] * 4, out_specs=vmem, out_sha...  57 us
    pallas_call x1, Pallas kernels, gram_terms(): pl.pallas_call(gram_kernel, in_specs=[pl.BlockSpec(memory_space=pltpu.SME...  53.1 us
    all_to_all x1, waiting for transfers between devices, on_device(): lax.all_to_all(weights, 'usr', split_axis=0, concat_axis=0, tiled=True)  34.8 us
    reduce_scatter x1, waiting for transfers between devices, on_device(): packed = lax.psum_scatter(packed, 'grp', scatter_dimension=0, tiled=True)  32 us
    pallas_call x1, Pallas kernels, make_stats(): pl.pallas_call(functools.partial(stats_kernel, n // peers), in_specs=[sme...  11.6 us
    unnamed x22, local copies, waits for them, and re-layouts  9.72 us
  transfers between devices with their start and end apart: 4, of which 4 were waited for; matrix products, arithmetic and copies ran while one was open for 0% of the time, Pallas kernels for 2%

profile of v2, /device:TPU:1, one launch (start us, length us, event | category | flops | bytes accessed | tf_op | source)
XLA Modules:
  0.0 375.0 jit_solution(8956095973032142638)
XLA Ops:
  7.2 0.0 copy-start
  7.2 0.8 copy.14
  8.0 0.1 reshape_squeeze.3.listed
  8.1 0.7 fusion
  8.8 0.1 reshape.27.live
  8.9 0.0 copy-start.4
  8.9 1.6 copy-done.4
  10.5 2.0 pick_blocks.1
  12.5 2.7 copy-done.1
  15.1 9.6 %all-to-all-start = ((bf16[96,128,256]{2,1,0:T(8,128)(2,1)}), bf16[96,128,256]{2,1,0:T(8,128)(2,1)}, u32[]{:S(2)}, u32[]{:S(2)}) async-start(bf16[96,128,256]{2,1,0:T(8,128)(2,1)} %copy-done.1), calls=%async_computation | async-start | bytes 12582912 | tf_op jit(solution)/shard_map/all_to_all | solution.py:318
  24.8 0.0 reduce-scatter.2.cloned.1.call-start
  24.9 6.1 %make_weights.1 = f32[96,56,128]{2,1,0:T(8,128)S(1)} custom-call(s32[56,768]{1,0:T(8,128)S(1)} %bitcast.15, bf16[56,768]{1,0:T(8,128)(2,1)S(1)} %bitcast.17), custom_call_target="tpu_custom_call" | custom-call | tf_op jit(solution)/shard_map/make_weights/pallas_call | solution.py:83
  31.0 0.0 copy-start.2
  31.0 1.5 copy-done.2
  32.5 65.2 %all-to-all-done = bf16[96,128,256]{2,1,0:T(8,128)(2,1)} async-done(((bf16[96,128,256]{2,1,0:T(8,128)(2,1)}), bf16[96,128,256]{2,1,0:T(8,128)(2,1)}, u32[]{:S(2)}, u32[]{:S(2)}) %all-to-all-start) | async-done | bytes 6291488 | tf_op jit(solution)/shard_map/all_to_all | solution.py:318
  97.7 53.1 %gram_terms.1 = f32[56,264,128]{2,1,0:T(8,128)} custom-call(s32[43008]{0:T(1024)S(1)} %mul.15.refs, bf16[12288,256]{1,0:T(8,128)(2,1)} %bitcast.4.table, f32[56,768]{1,0:T(8,128)S(1)} %bitcast_convert_fusion.values), custom_call_target="tpu_custom_call" | custom-call | tf_op jit(solution)/shard_map/gram_terms/pallas_call | solution.py:157
  150.8 0.0 reduce-scatter.2.cloned.1.call-update
  150.8 0.0 copy-start.8
  150.8 0.0 copy-start.9
  150.8 9.1 %all-to-all-start.1 = ((f32[96,56,128]{2,1,0:T(8,128)}), f32[96,56,128]{2,1,0:T(8,128)S(1)}, u32[]{:S(2)}, u32[]{:S(2)}) async-start(f32[96,56,128]{2,1,0:T(8,128)} %copy-done.2), calls=%async_computation.2 | async-start | bytes 5505024 | tf_op jit(solution)/shard_map/all_to_all | solution.py:321
  159.9 0.0 all-gather.3.cloned.1.call-start
  160.0 0.1 copy.16
  160.1 34.8 %all-to-all-done.1.weights = f32[96,56,128]{2,1,0:T(8,128)S(1)} async-done(((f32[96,56,128]{2,1,0:T(8,128)}), f32[96,56,128]{2,1,0:T(8,128)S(1)}, u32[]{:S(2)}, u32[]{:S(2)}) %all-to-all-start.1) | async-done | bytes 2752544 | tf_op jit(solution)/shard_map/all_to_all | solution.py:321
  194.9 32.0 %reduce-scatter.2.cloned.1.call-done.packed = f32[14,264,128]{2,1,0:T(8,128)} async-done(((f32[56,264,128]{2,1,0:T(8,128)}), f32[14,264,128]{2,1,0:T(8,128)}) %reduce-scatter.2.cloned.1.call-update) | async-done | bytes 1892368 | tf_op jit(solution)/shard_map/reduce_scatter | solution.py:324
  227.0 1.5 copy-done.5
  228.5 57.0 %solve_users.1 = f32[14,256]{1,0:T(8,128)} custom-call(f32[14,264,128]{2,1,0:T(8,128)S(1)} %copy-done.5, f32[256,14]{1,0:T(8,128)S(1)} %bitcast.16, f32[256,256]{1,0:T(8,128)S(1)} %copy-done.8, f32[1,256]{1,0:T(1,128)S(1)} %bitcast.18), custom_call_target="tpu_custom_call" | custom-call | tf_op jit(solution)/shard_map/solve_users/pallas_call | solution.py:258
  285.6 0.0 all-gather.3.cloned.1.call-update
  285.6 65.5 %all-gather.3.cloned.1.call-done = f32[128,14,256]{2,1,0:T(8,128)} async-done(((f32[1,14,256]{2,1,0:T(8,128)}), f32[128,14,256]{2,1,0:T(8,128)}) %all-gather.3.cloned.1.call-update) | async-done | bytes 1835024 | tf_op jit(solution)/shard_map/all_gather | solution.py:329
  351.0 2.6 reshape.26.samples
  353.7 1.4 dynamic-slice_bitcast_fusion
  355.1 1.5 copy-done.3
  356.6 11.6 %make_stats.1 = f32[32,128,256]{2,1,0:T(8,128)} custom-call(s32[96]{0:T(128)S(1)} %reshape_squeeze.3.listed, s32[96]{0:T(128)S(1)} %reshape.27.live, f32[96,56,128]{2,1,0:T(8,128)S(1)} %all-to-all-done.1.weights, f32[32,56,256]{2,1,0:T(8,128)S(1)} %copy-done.3), custom_call_target="tpu_custom_call" | custom-call | tf_op jit(solution)/shard_map/make_stats/pallas_call | solution.py:297
  (14 shorter events, 0.1 us)
Async XLA Ops:
  7.2 152.8 %copy-start = (f32[56,256]{1,0:T(8,128)S(1)}, f32[56,256]{1,0:T(8,128)}, u32[]{:S(2)}) copy-start(f32[56,256]{1,0:T(8,128)} %param.13) | copy-start | bytes 172036
  8.9 1.6 copy-start.4
  12.5 2.7 copy-start.1
  15.1 9.7 %copy-start.6 = (s32[1,56,768]{2,1,0:T(8,128)S(1)}, s32[1,56,768]{2,1,0:T(8,128)}, u32[]{:S(2)}) copy-start(s32[1,56,768]{2,1,0:T(8,128)} %param.11) | copy-start | bytes 516100
  15.1 9.7 %copy-start.7 = (bf16[1,56,768]{2,1,0:T(8,128)(2,1)S(1)}, bf16[1,56,768]{2,1,0:T(8,128)(2,1)}, u32[]{:S(2)}) copy-start(bf16[1,56,768]{2,1,0:T(8,128)(2,1)} %param.12) | copy-start | bytes 258052
  15.1 82.6 %all-to-all-start = ((bf16[96,128,256]{2,1,0:T(8,128)(2,1)}), bf16[96,128,256]{2,1,0:T(8,128)(2,1)}, u32[]{:S(2)}, u32[]{:S(2)}) async-start(bf16[96,128,256]{2,1,0:T(8,128)(2,1)} %copy-done.1), calls=%async_computation | async-start | bytes 12582912 | tf_op jit(solution)/shard_map/all_to_all | solution.py:318
  24.8 202.2 %reduce-scatter.2.cloned.1.call-start = ((), (), s32[]{:S(2)}) async-start(), calls=%async_computation.3 | async-start | bytes 9461760 | tf_op jit(solution)/shard_map/reduce_scatter | solution.py:324
  31.0 1.5 copy-start.2
  150.8 76.2 %copy-start.8 = (f32[256,256]{1,0:T(8,128)S(1)}, f32[256,256]{1,0:T(8,128)}, u32[]{:S(2)}) copy-start(f32[256,256]{1,0:T(8,128)} %prior.1) | copy-start | bytes 786436
  150.8 76.2 %copy-start.9 = (f32[256]{0:T(256)S(1)}, f32[256]{0:T(256)}, u32[]{:S(2)}) copy-start(f32[256]{0:T(256)} %param.15) | copy-start | bytes 3076
  150.8 44.1 %all-to-all-start.1 = ((f32[96,56,128]{2,1,0:T(8,128)}), f32[96,56,128]{2,1,0:T(8,128)S(1)}, u32[]{:S(2)}, u32[]{:S(2)}) async-start(f32[96,56,128]{2,1,0:T(8,128)} %copy-done.2), calls=%async_computation.2 | async-start | bytes 5505024 | tf_op jit(solution)/shard_map/all_to_all | solution.py:321
  159.9 191.1 %all-gather.3.cloned.1.call-start = ((), (), s32[]{:S(2)}) async-start(), calls=%async_computation.4 | async-start | bytes 2113536 | tf_op jit(solution)/shard_map/all_gather | solution.py:329
  227.0 1.5 copy-start.5
  355.1 1.5 copy-start.3
Sparse Core Ops, SparseCore 0:
  150.9 76.0 reduce-scatter.1
  285.7 65.2 all-gather.2

commit v3 on v2

--- a/solution.py
+++ b/solution.py
@@ -11,6 +11,7 @@
 F32 = jnp.float32
 BF16 = jnp.bfloat16
 MIB = 2**20
+MESH = pl.DeviceIdType.MESH
 
 
 def iota(shape, dim):
@@ -95,7 +96,7 @@
     slots = picked.shape[0] // 2
     unroll = 16
     for base in range(0, slots, unroll):
-        got = [wide[pl.ds(pl.multiple_of(refs[user * slots + base + j], 2), 2), :] for j in range(unroll)]
+        got = [wide[pl.ds(refs[user * slots + base + j], 2), :] for j in range(unroll)]
         for j in range(unroll):
             picked[2 * (base + j) : 2 * (base + j) + 2, :] = got[j]
 
@@ -119,10 +120,16 @@
     store(256, jnp.where(row == 0, diag, tail))
 
 
-def gram_kernel(refs, table, values, out, wide, even, odd):
+def gram_kernel(refs, table, values, out, wide, even, odd, stage, near, far, send_sem, recv_sem):
     rows = table.shape[0]
-    users = out.shape[0]
-    chunk = 128
+    share, height, _ = out.shape
+    chunk, cut = 128, near.shape[2] // 16 * 8
+    me, ring = lax.axis_index("grp"), 4
+    after, before = (me + 1) % ring, (me + ring - 1) % ring
+
+    barrier = pltpu.get_barrier_semaphore()
+    for peer in (after, before):
+        pl.semaphore_signal(barrier, inc=1, device_id={"grp": peer}, device_id_type=MESH)
 
     def widen(i, carry):
         part = table[pl.ds(i * chunk, chunk), :].astype(F32)
@@ -131,36 +138,108 @@
         return carry
 
     lax.fori_loop(0, rows // chunk, widen, 0)
-
-    def terms(picked, u):
+    pl.semaphore_wait(barrier, 2)
+
+    def copy(j, kind):
+        if kind == 0:
+            src, dst, peer = stage.at[2, j, :cut], far.at[0, j, :cut], after
+        elif kind == 1:
+            src, dst, peer = stage.at[2, j, cut:], far.at[1, j, cut:], before
+        elif kind == 2:
+            src, dst, peer = stage.at[1, j], near.at[0, j], after
+        else:
+            src, dst, peer = stage.at[3, j], near.at[1, j], before
+        return pltpu.make_async_remote_copy(
+            src_ref=src,
+            dst_ref=dst,
+            send_sem=send_sem.at[j, kind],
+            recv_sem=recv_sem.at[j, kind],
+            device_id={"grp": peer},
+            device_id_type=MESH,
+        )
+
+    def user(j, kind):
+        return (me + kind) % ring * share + j
+
+    def terms(picked, j, kind):
         def store(at, part):
-            out[u, at : at + part.shape[0], :] = part
-
-        packed_terms(picked, values[pl.ds(u, 1), :].astype(BF16), store)
-
-    gather_rows(wide, even, refs, 0)
-
-    def pair(i, carry):
-        gather_rows(wide, odd, refs, 2 * i + 1)
-        terms(even, 2 * i)
-        gather_rows(wide, even, refs, lax.min(2 * i + 2, users - 1))
-        terms(odd, 2 * i + 1)
+            stage[kind, j, at : at + part.shape[0], :] = part
+
+        packed_terms(picked, values[pl.ds(user(j, kind), 1), :].astype(BF16), store)
+
+    def pass_on(j):
+        copy(j, 0).wait_recv()
+        stage[1, j, :cut, :] = stage[1, j, :cut, :] + far[0, j, :cut, :]
+        copy(j, 2).start()
+        copy(j, 1).wait_recv()
+        stage[3, j, cut:, :] = stage[3, j, cut:, :] + far[1, j, cut:, :]
+        copy(j, 3).start()
+
+    def finish(j):
+        copy(j, 2).wait_recv()
+        copy(j, 3).wait_recv()
+        out[j] = stage[0, j] + near[0, j] + near[1, j]
+
+    gather_rows(wide, even, refs, user(0, 2))
+
+    def turn(j, carry):
+        gather_rows(wide, odd, refs, user(j, 1))
+        terms(even, j, 2)
+        copy(j, 0).start()
+        copy(j, 1).start()
+        gather_rows(wide, even, refs, user(j, 3))
+        terms(odd, j, 1)
+        gather_rows(wide, odd, refs, user(j, 0))
+        terms(even, j, 3)
+        gather_rows(wide, even, refs, user((j + 1) % share, 2))
+        terms(odd, j, 0)
+
+        @pl.when(j >= 1)
+        def _():
+            pass_on(j - 1)
+
+        @pl.when(j >= 2)
+        def _():
+            finish(j - 2)
+
         return carry
 
-    lax.fori_loop(0, users // 2, pair, 0)
+    lax.fori_loop(0, share, turn, 0)
+    pass_on(share - 1)
+    finish(share - 2)
+    finish(share - 1)
+
+    def drain(j, carry):
+        for kind in range(4):
+            copy(j, kind).wait_send()
+        return carry
+
+    lax.fori_loop(0, share, drain, 0)
 
 
 def gram_terms(table, refs, values):
     users, slots = refs.shape
     rows, rank = table.shape
+    ring, height = 4, 264
+    share = users // ring
     vmem = pl.BlockSpec(memory_space=pltpu.VMEM)
     return pl.pallas_call(
         gram_kernel,
         in_specs=[pl.BlockSpec(memory_space=pltpu.SMEM), vmem, vmem],
         out_specs=vmem,
-        out_shape=jax.ShapeDtypeStruct((users, 264, 128), F32),
-        scratch_shapes=[pltpu.VMEM((2 * rows, 128), F32)] + [pltpu.VMEM((2 * slots, 128), F32)] * 2,
-        compiler_params=pltpu.CompilerParams(vmem_limit_bytes=48 * MIB),
+        out_shape=jax.ShapeDtypeStruct((share, height, 128), F32),
+        scratch_shapes=[
+            pltpu.VMEM((2 * rows, 128), F32),
+            pltpu.VMEM((2 * slots, 128), F32),
+            pltpu.VMEM((2 * slots, 128), F32),
+            pltpu.VMEM((ring, share, height, 128), F32),
+            pltpu.VMEM((2, share, height, 128), F32),
+            pltpu.VMEM((2, share, height, 128), F32),
+            pltpu.SemaphoreType.DMA((share, 4)),
+            pltpu.SemaphoreType.DMA((share, 4)),
+        ],
+        compiler_params=pltpu.CompilerParams(vmem_limit_bytes=56 * MIB, collective_id=0, has_side_effects=True),
+        cost_estimate=pl.CostEstimate(flops=60 * 10**9, bytes_accessed=200 * MIB, transcendentals=0),
         name="gram_terms",
     )((2 * refs).reshape(users * slots), table, values.astype(F32))
 
@@ -271,11 +350,83 @@
     )(packed, noise.T, prior, shift.reshape(1, rank))
 
 
-def stats_kernel(cols, listed, live, weights, samples, out):
+def share_kernel(own, out, first_send, first_recv, send_sem, recv_sem, twin_send, twin_recv):
+    g, u = lax.axis_index("grp"), lax.axis_index("usr")
+    ring, side = 4, 4
+    core, x, z = u % 2, u // 2 % side, u // (2 * side)
+    twin = u + 1 - 2 * core
+    moves = [(a, b) for a in range(side) for b in range(side) if a or b]
+
+    def place(dz, dx):
+        return (z + dz) % side * (2 * side) + (x + dx) % side * 2 + core
+
+    barrier = pltpu.get_barrier_semaphore()
+    for o in range(1, ring):
+        pl.semaphore_signal(barrier, inc=1, device_id={"grp": (g + o) % ring}, device_id_type=MESH)
+    for move in moves:
+        pl.semaphore_signal(barrier, inc=1, device_id={"usr": place(*move)}, device_id_type=MESH)
+    pl.semaphore_signal(barrier, inc=1, device_id={"usr": twin}, device_id_type=MESH)
+    pl.semaphore_wait(barrier, ring + len(moves))
+
+    def remote(src, dst, send, recv, peer):
+        return pltpu.make_async_remote_copy(
+            src_ref=src, dst_ref=dst, send_sem=send, recv_sem=recv, device_id=peer, device_id_type=MESH
+        )
+
+    first = [
+        remote(own, out.at[u, g], first_send.at[o - 1], first_recv.at[o - 1], {"grp": (g + o) % ring})
+        for o in range(1, ring)
+    ]
+    for c in first:
+        c.start()
+    out[u, g] = own[...]
+    for o in range(1, ring):
+        src = (g + ring - o) % ring
+        remote(own, out.at[u, src], first_send.at[o - 1], first_recv.at[o - 1], {"grp": src}).wait_recv()
+    slab = out.at[u]
+    second = [
+        remote(slab, slab, send_sem.at[k], recv_sem.at[k], {"usr": place(*move)}) for k, move in enumerate(moves)
+    ]
+    for c in second:
+        c.start()
+    to_twin = [remote(slab, slab, twin_send.at[len(moves)], twin_recv.at[len(moves)], {"usr": twin})]
+    to_twin[0].start()
+    for k, (dz, dx) in enumerate(moves):
+        src = out.at[place(-dz + side, -dx + side)]
+        remote(src, src, send_sem.at[k], recv_sem.at[k], {"usr": twin}).wait_recv()
+        c = remote(src, src, twin_send.at[k], twin_recv.at[k], {"usr": twin})
+        c.start()
+        to_twin.append(c)
+    for c in to_twin:
+        c.wait_recv()
+    for c in first + second + to_twin:
+        c.wait_send()
+
+
+def share_samples(own):
+    share, rank = own.shape
+    peers, ring = lax.axis_size("usr"), lax.axis_size("grp")
+    vmem = pl.BlockSpec(memory_space=pltpu.VMEM)
+    dma = pltpu.SemaphoreType.DMA
+    return pl.pallas_call(
+        share_kernel,
+        in_specs=[vmem],
+        out_specs=vmem,
+        out_shape=jax.ShapeDtypeStruct((peers, ring, share, rank), F32),
+        scratch_shapes=[dma((ring - 1,)), dma((ring - 1,)), dma((15,)), dma((15,)), dma((16,)), dma((16,))],
+        compiler_params=pltpu.CompilerParams(vmem_limit_bytes=32 * MIB, collective_id=1, has_side_effects=True),
+        name="share_samples",
+    )(own)
+
+
+def stats_kernel(cols, listed, live, weights, samples, out, held):
     out[...] = jnp.zeros_like(out)
+    parts, share = samples.shape[1:3]
 
     def device(d, carry):
-        hi, lo = split(samples[d])
+        for g in range(parts):
+            held[g * share : (g + 1) * share, :] = samples[d, g]
+        hi, lo = split(held[...])
         other = jnp.concatenate([hi, lo, hi, lo], axis=0).astype(BF16)
         for c in range(cols):
             i = d * cols + c
@@ -291,7 +442,7 @@
 
 def make_stats(weights, samples, listed, live, owned):
     n, users, height = weights.shape
-    peers, _, rank = samples.shape
+    peers, _, _, rank = samples.shape
     vmem = pl.BlockSpec(memory_space=pltpu.VMEM)
     smem = pl.BlockSpec(memory_space=pltpu.SMEM)
     return pl.pallas_call(
@@ -299,6 +450,7 @@
         in_specs=[smem, smem, vmem, vmem],
         out_specs=vmem,
         out_shape=jax.ShapeDtypeStruct((owned, height, rank), F32),
+        scratch_shapes=[pltpu.VMEM((users, rank), F32)],
         compiler_params=pltpu.CompilerParams(vmem_limit_bytes=32 * MIB),
         name="make_stats",
     )(listed, live, weights, samples)
@@ -321,13 +473,12 @@
     gathered = lax.all_to_all(weights, "usr", split_axis=0, concat_axis=0, tiled=True)
 
     packed = gram_terms(incoming.reshape(n * height, rank), refs, values)
-    packed = lax.psum_scatter(packed, "grp", scatter_dimension=0, tiled=True)
     packed, gathered = lax.optimization_barrier((packed, gathered))
     share = packed.shape[0]
     draws = lax.dynamic_slice_in_dim(noise, lax.axis_index("grp") * share, share, 0)
-    own = solve_users(packed, draws, prior_prec, prior_shift)
-    everyone = lax.all_gather(own, ("usr", "grp"), axis=0, tiled=True).reshape(peers, refs.shape[0], rank)
+    everyone = share_samples(solve_users(packed, draws, prior_prec, prior_shift))
     samples = lax.dynamic_index_in_dim(everyone, lax.axis_index("usr"), 0, keepdims=False)
+    samples = samples.reshape(refs.shape[0], rank)
     stats = make_stats(gathered, everyone, listed, live, owned)
     return (samples, stats[None])
 

time: 376 us -> 272 us (0.72)
  waiting for transfers between devices: 198 us -> 63.8 us
  Pallas kernels: 130 us -> 177 us
  between operations: 14.2 us -> 0.81 us
  local copies, waits for them, and re-layouts: 14 us -> 9.71 us
    all_gather x1 -> x0, waiting for transfers between devices: 65.5 us -> none  [on_device(): lax.all_gather(own, ('usr', 'grp'), axis=0, tiled=True)]
    all_to_all x1, waiting for transfers between devices: 34.8 us -> 0.01 us  [on_device(): lax.all_to_all(weights, 'usr', split_axis=0, concat_axis=0, tiled=True)]
    reduce_scatter x1 -> x0, waiting for transfers between devices: 32 us -> none  [on_device(): packed = lax.psum_scatter(packed, 'grp', scatter_dimension=0, tiled=True)]
    pallas_call x0 -> x1, Pallas kernels: none -> 26.4 us  [share_samples(): pl.pallas_call(share_kernel, in_specs=[vmem], out_specs=vmem, out_shape=j...]
    pallas_call x1, Pallas kernels: 53.1 us -> 74.4 us  [gram_terms(): pl.pallas_call(gram_kernel, in_specs=[pl.BlockSpec(memory_space=pltpu.SME...]
    unnamed x22 -> x20, local copies, waits for them, and re-layouts: 9.72 us -> 8.17 us
  transfers between devices with their start and end apart: 4 -> 2, of which waited for: 4 -> 1; matrix products, arithmetic and copies ran while one was open for 0% -> 1% of each run, Pallas kernels for 2% -> 30%
where the time goes in v3:
time: 272 us; the launch traced here: 271 us
  Pallas kernels  177 us (65%)
  waiting for transfers between devices  63.8 us (23%)
  starting transfers between devices  18.6 us (7%)
  local copies, waits for them, and re-layouts  9.71 us (4%)
    pallas_call x1, Pallas kernels, gram_terms(): pl.pallas_call(gram_kernel, in_specs=[pl.BlockSpec(memory_space=pltpu.SME...  74.4 us
    all_to_all x1, waiting for transfers between devices, on_device(): lax.all_to_all(outgoing, 'usr', split_axis=0, concat_axis=0, tiled=True)  63.8 us
    pallas_call x1, Pallas kernels, solve_users(): pl.pallas_call(solve_kernel, in_specs=[vmem] * 4, out_specs=vmem, out_sha...  56.4 us
    pallas_call x1, Pallas kernels, share_samples(): pl.pallas_call(share_kernel, in_specs=[vmem], out_specs=vmem, out_shape=j...  26.4 us
    pallas_call x1, Pallas kernels, make_stats(): pl.pallas_call(functools.partial(stats_kernel, n // peers), in_specs=[sme...  11.7 us
    all_to_all x1, starting transfers between devices, on_device(): lax.all_to_all(outgoing, 'usr', split_axis=0, concat_axis=0, tiled=True)  9.61 us
    all_to_all x1, starting transfers between devices, on_device(): lax.all_to_all(weights, 'usr', split_axis=0, concat_axis=0, tiled=True)  8.95 us
    unnamed x20, local copies, waits for them, and re-layouts  8.17 us
  transfers between devices with their start and end apart: 2, of which 1 were waited for; matrix products, arithmetic and copies ran while one was open for 1% of the time, Pallas kernels for 30%

profile of v3, /device:TPU:1, one launch (start us, length us, event | category | flops | bytes accessed | tf_op | source)
XLA Modules:
  0.0 271.3 jit_solution(7749607381485067340)
XLA Ops:
  0.6 0.0 copy-start
  0.6 0.7 fusion
  1.4 0.1 reshape.28.live
  1.5 0.8 copy.12
  2.3 0.1 reshape_squeeze.3.listed
  2.4 0.0 copy-start.3
  2.4 1.6 copy-done.3
  4.0 2.0 pick_blocks.1
  5.9 0.0 copy-start.1
  6.0 2.6 copy-done.1
  8.6 9.6 %all-to-all-start = ((bf16[96,128,256]{2,1,0:T(8,128)(2,1)}), bf16[96,128,256]{2,1,0:T(8,128)(2,1)}, u32[]{:S(2)}, u32[]{:S(2)}) async-start(bf16[96,128,256]{2,1,0:T(8,128)(2,1)} %copy-done.1), calls=%async_computation | async-start | bytes 12582912 | tf_op jit(solution)/shard_map/all_to_all | solution.py:470
  18.2 0.0 copy-done
  18.2 0.1 copy.14
  18.4 0.0 copy-done.5
  18.4 0.7 mul.15.refs
  19.1 0.0 copy-done.6
  19.1 6.1 %make_weights.1 = f32[96,56,128]{2,1,0:T(8,128)S(1)} custom-call(s32[56,768]{1,0:T(8,128)S(1)} %bitcast.12, bf16[56,768]{1,0:T(8,128)(2,1)S(1)} %bitcast.14), custom_call_target="tpu_custom_call" | custom-call | tf_op jit(solution)/shard_map/make_weights/pallas_call | solution.py:84
  25.2 0.0 copy-start.2
  25.2 1.5 copy-done.2
  26.7 0.7 bitcast_convert_fusion.values
  27.4 63.8 %all-to-all-done = bf16[96,128,256]{2,1,0:T(8,128)(2,1)} async-done(((bf16[96,128,256]{2,1,0:T(8,128)(2,1)}), bf16[96,128,256]{2,1,0:T(8,128)(2,1)}, u32[]{:S(2)}, u32[]{:S(2)}) %all-to-all-start) | async-done | bytes 6291488 | tf_op jit(solution)/shard_map/all_to_all | solution.py:470
  91.2 8.9 %all-to-all-start.1 = ((f32[96,56,128]{2,1,0:T(8,128)}), f32[96,56,128]{2,1,0:T(8,128)S(1)}, u32[]{:S(2)}, u32[]{:S(2)}) async-start(f32[96,56,128]{2,1,0:T(8,128)} %copy-done.2), calls=%async_computation.1 | async-start | bytes 5505024 | tf_op jit(solution)/shard_map/all_to_all | solution.py:473
  100.1 0.0 copy-start.7
  100.1 0.0 copy-start.8
  100.1 74.4 %gram_terms.1.packed = f32[14,264,128]{2,1,0:T(8,128)} custom-call(s32[43008]{0:T(1024)} %mul.15.refs, bf16[12288,256]{1,0:T(8,128)(2,1)} %bitcast.4.table, f32[56,768]{1,0:T(8,128)} %bitcast_convert_fusion.values), custom_call_target="tpu_custom_call" | custom-call | flops 60000002048 | bytes 209715200 | tf_op jit(solution)/shard_map/gram_terms/pallas_call | solution.py:226
  174.6 0.0 all-to-all-done.1.weights
  174.6 0.0 copy-done.7
  174.6 1.5 copy-done.4
  176.1 56.4 %solve_users.1.own = f32[14,256]{1,0:T(8,128)S(1)} custom-call(f32[14,264,128]{2,1,0:T(8,128)S(1)} %copy-done.4, f32[256,14]{1,0:T(8,128)S(1)} %bitcast.13, f32[256,256]{1,0:T(8,128)S(1)} %copy-done.7, f32[1,256]{1,0:T(1,128)S(1)} %bitcast.15), custom_call_target="tpu_custom_call" | custom-call | tf_op jit(solution)/shard_map/solve_users/pallas_call | solution.py:337
  232.6 26.4 %share_samples.1.samples = f32[32,4,14,256]{3,2,1,0:T(8,128)S(1)} custom-call(f32[14,256]{1,0:T(8,128)S(1)} %solve_users.1.own), custom_call_target="tpu_custom_call" | custom-call | tf_op jit(solution)/shard_map/share_samples/pallas_call | solution.py:411
  259.0 11.7 %make_stats.1 = f32[32,128,256]{2,1,0:T(8,128)} custom-call(s32[96]{0:T(128)S(1)} %reshape_squeeze.3.listed, s32[96]{0:T(128)S(1)} %reshape.28.live, f32[96,56,128]{2,1,0:T(8,128)S(1)} %all-to-all-done.1.weights, f32[32,4,14,256]{3,2,1,0:T(8,128)S(1)} %share_samples.1.samples), custom_call_target="tpu_custom_call" | custom-call | tf_op jit(solution)/shard_map/make_stats/pallas_call | solution.py:448
  270.7 0.6 reshape.27
  (7 shorter events, 0.0 us)
Async XLA Ops:
  0.6 17.6 %copy-start = (f32[56,256]{1,0:T(8,128)S(1)}, f32[56,256]{1,0:T(8,128)}, u32[]{:S(2)}) copy-start(f32[56,256]{1,0:T(8,128)} %param.13) | copy-start | bytes 172036
  2.4 1.6 copy-start.3
  5.9 2.6 copy-start.1
  8.6 9.8 %copy-start.5 = (s32[1,56,768]{2,1,0:T(8,128)S(1)}, s32[1,56,768]{2,1,0:T(8,128)}, u32[]{:S(2)}) copy-start(s32[1,56,768]{2,1,0:T(8,128)} %param.11) | copy-start | bytes 516100
  8.6 10.5 %copy-start.6 = (bf16[1,56,768]{2,1,0:T(8,128)(2,1)S(1)}, bf16[1,56,768]{2,1,0:T(8,128)(2,1)}, u32[]{:S(2)}) copy-start(bf16[1,56,768]{2,1,0:T(8,128)(2,1)} %param.12) | copy-start | bytes 258052
  8.6 82.6 %all-to-all-start = ((bf16[96,128,256]{2,1,0:T(8,128)(2,1)}), bf16[96,128,256]{2,1,0:T(8,128)(2,1)}, u32[]{:S(2)}, u32[]{:S(2)}) async-start(bf16[96,128,256]{2,1,0:T(8,128)(2,1)} %copy-done.1), calls=%async_computation | async-start | bytes 12582912 | tf_op jit(solution)/shard_map/all_to_all | solution.py:470
  25.2 1.5 copy-start.2
  91.2 83.4 %all-to-all-start.1 = ((f32[96,56,128]{2,1,0:T(8,128)}), f32[96,56,128]{2,1,0:T(8,128)S(1)}, u32[]{:S(2)}, u32[]{:S(2)}) async-start(f32[96,56,128]{2,1,0:T(8,128)} %copy-done.2), calls=%async_computation.1 | async-start | bytes 5505024 | tf_op jit(solution)/shard_map/all_to_all | solution.py:473
  100.1 74.5 %copy-start.7 = (f32[256,256]{1,0:T(8,128)S(1)}, f32[256,256]{1,0:T(8,128)}, u32[]{:S(2)}) copy-start(f32[256,256]{1,0:T(8,128)} %prior.1) | copy-start | bytes 786436
  100.1 74.5 %copy-start.8 = (f32[256]{0:T(256)S(1)}, f32[256]{0:T(256)}, u32[]{:S(2)}) copy-start(f32[256]{0:T(256)} %param.15) | copy-start | bytes 3076
  174.6 1.5 copy-start.4

commit v4 on v3

--- a/solution.py
+++ b/solution.py
@@ -23,10 +23,17 @@
     return hi, x - hi
 
 
-def stacked(x):
-    hi, lo = split(x)
-    left = jnp.concatenate([hi, hi, lo, lo], axis=0).astype(BF16)
-    right = jnp.concatenate([hi, lo, hi, lo], axis=0).astype(BF16)
+def split3(x):
+    hi = x.astype(BF16).astype(F32)
+    rest = x - hi
+    mid = rest.astype(BF16).astype(F32)
+    return hi, mid, rest - mid
+
+
+def stacked3(x):
+    hi, mid, low = split3(x)
+    left = jnp.concatenate([hi, hi, mid, hi, low, mid], axis=0).astype(BF16)
+    right = jnp.concatenate([hi, mid, hi, low, hi, mid], axis=0).astype(BF16)
     return left, right
 
 
@@ -248,7 +255,7 @@
     users = packed.shape[0]
     rank = prior.shape[0]
     half = rank // 2
-    step, outer = 8, 64
+    step = 32
 
     r, c = iota((half, half), 0), iota((half, half), 1)
     for m in range(users):
@@ -261,73 +268,81 @@
         mats[m, :half, :half] = prior[:half, :half] + ALPHA * first
         mats[m, :half, half:] = prior[:half, half:] + ALPHA * cross
         mats[m, half:, half:] = prior[half:, half:] + ALPHA * last
-        mats[m, half:, :half] = jnp.zeros((half, half), F32)
         right[m, 0:1, :half] = ALPHA * packed[m, rank + 1 : rank + 2, :] + shift[:, :half]
         right[m, 0:1, half:] = ALPHA * packed[m, rank + 2 : rank + 3, :] + shift[:, half:]
 
-    sub = iota((1, step, 128), 1)
-    lane = iota((1, step, 128), 2)
-    wide_lane = iota((step, rank), 1)
-    unit = jnp.where(lane == sub + step, 1.0, 0.0)
-
-    for o in range(rank // outer):
-        lo = o * outer
-
-        def panel(i, carry, lo=lo):
-            k0 = pl.multiple_of(lo + i * step, step)
-            rows = mats[:, pl.ds(k0, step), :]
-            turn = (rank - k0) % rank
-            aux = jnp.stack([pltpu.roll(rows[m], turn, 1)[:, :128] for m in range(users)])
-            aux = jnp.where(lane < step, aux, unit)
-            for k in range(step):
-                col = aux[:, :, k : k + 1]
-                factor = jnp.where(sub[:, :, :1] > k, col / col[:, k : k + 1, :], 0.0)
-                aux = aux - factor * aux[:, k : k + 1, :]
-                rows = rows - factor * rows[:, k : k + 1, :]
-            pivots = jnp.sum(jnp.where(lane == sub, aux, 0.0), axis=2, keepdims=True)
-            scale = lax.rsqrt(pivots)
-            rows = rows * scale
-            inverse = jnp.where((lane >= step) & (lane < 2 * step), aux * scale, 0.0)
-            mats[:, pl.ds(k0, step), :] = rows
-            noise = noise_cols[pl.ds(k0, step), :]
-            for m in range(users):
-                spread = jnp.concatenate([inverse[m], jnp.zeros((step, rank - 128), F32)], axis=1)
-                spread = pltpu.roll(spread, (k0 + rank - step) % rank, 1)
-                back[m, pl.ds(k0, step), :] = spread
-                given = right[m, 0:1, :]
-                y = jnp.sum(spread * given, axis=1, keepdims=True)
-                right[m, 0:1, :] = given - jnp.sum(y * rows[m], axis=0, keepdims=True)
-                sums[m, pl.ds(k0, step), :] = jnp.broadcast_to(y + noise[:, m : m + 1], (step, 128))
-                hi, rest = split(rows[m])
-                later = wide_lane >= k0 + step
-                left = jnp.concatenate([hi, hi, rest, rest], axis=0)
-                left = jnp.where(jnp.concatenate([later] * 4, axis=0), left, 0.0)[:, lo : lo + outer].astype(BF16)
-                other = jnp.concatenate([hi, rest, hi, rest], axis=0).astype(BF16)
-                mats[m, lo : lo + outer, :] = mats[m, lo : lo + outer, :] - dot_tn(left, other)
-            return carry
-
-        lax.fori_loop(0, outer // step, panel, 0)
-        if lo + outer < rank:
-            start = (lo + outer) // 128 * 128
-
-            def trail(m, carry, lo=lo, start=start):
-                left, other = stacked(mats[m, lo : lo + outer, :])
-                mats[m, lo + outer :, start:] = mats[m, lo + outer :, start:] - dot_tn(
-                    left[:, lo + outer :], other[:, start:]
-                )
-                return carry
-
-            lax.fori_loop(0, users, trail, 0)
-
-    def backward(i, x):
-        k0 = pl.multiple_of(rank - step - i * step, step)
-        rows = mats[:, pl.ds(k0, step), :]
-        rest = sums[:, pl.ds(k0, step), :][:, :, :1] - jnp.sum(rows * x, axis=2, keepdims=True)
-        return x + jnp.sum(back[:, pl.ds(k0, step), :] * rest, axis=1, keepdims=True)
-
-    x = lax.fori_loop(0, rank // step, backward, jnp.zeros((users, 1, rank), F32))
+    sub = iota((1, 8, 128), 1)
+    lane = iota((1, 8, 128), 2)
+    tall_lane = iota((step, 128), 1)
+
+    def column(x, k):
+        return jnp.broadcast_to(x[:, :, k : k + 1], x.shape)
+
+    for k0 in range(0, rank, step):
+        tile, group = k0 // half * half, k0 % half // step
+        parts, pivots = [], []
+        for h in range(step // 8):
+            rows = mats[:, k0 + 8 * h : k0 + 8 * h + 8, tile : tile + half]
+            if group:
+                rows = jnp.stack([pltpu.roll(rows[m], half - group * step, 1) for m in range(users)])
+            unit = jnp.where(lane % step == sub + 8 * h, 1.0, 0.0)
+            parts.append(jnp.where(lane < step, rows, unit))
+            pivots.append(jnp.ones((users, 8, 128), F32))
+        for k in range(0, step, 2):
+            f, kk = k // 8, k % 8
+            ones = [column(parts[h], k) for h in range(f, step // 8)]
+            twos = [column(parts[h], k + 1) for h in range(f, step // 8)]
+            a, b, c = ones[0][:, kk : kk + 1, :], twos[0][:, kk : kk + 1, :], twos[0][:, kk + 1 : kk + 2, :]
+            low, high = parts[f][:, kk : kk + 1, :], parts[f][:, kk + 1 : kk + 2, :]
+            inv = 1.0 / (a * c - b * b)
+            ratio = b * (1.0 / a)
+            first = (c * low - b * high) * inv
+            second = (a * high - b * low) * inv
+            second_row = parts[f] - ratio * low
+            pivots[f] = jnp.where(sub == kk, a, jnp.where(sub == kk + 1, c - ratio * b, pivots[f]))
+            for h in range(f, step // 8):
+                new = parts[h] - ones[h - f] * first - twos[h - f] * second
+                if h == f:
+                    new = jnp.where(sub > kk + 1, new, jnp.where(sub == kk + 1, second_row, parts[h]))
+                parts[h] = new
+        scaled = [p * lax.rsqrt(v) for p, v in zip(parts, pivots)]
+        for m in range(users):
+            turn = jnp.concatenate([x[m] for x in scaled], axis=0)
+            hi, mid, low = split3(turn)
+            one = jnp.where(tall_lane < step, 0.0, jnp.where(tall_lane < 3 * step, hi, mid))
+            two = jnp.where(tall_lane < step, 0.0, jnp.where(tall_lane < 2 * step, hi, jnp.where(tall_lane < 3 * step, low, mid)))
+            left = jnp.concatenate([one, two], axis=1).astype(BF16)
+            hi, mid, low = split3(mats[m, k0 : k0 + step, tile:])
+            other = jnp.concatenate([hi, hi, mid, hi, hi, low, hi, mid], axis=0).astype(BF16)
+            rows = jnp.dot(left, other, preferred_element_type=F32)
+            mats[m, k0 : k0 + step, tile:] = rows
+            if not group:
+                turn = pltpu.roll(turn, half - step, 1)
+            keep = (tall_lane >= group * step) & (tall_lane < (group + 1) * step)
+            turn = jnp.where(keep, turn, 0.0)
+            back[m, k0 : k0 + step, :] = turn
+            y = jnp.sum(turn * right[m, 0:1, tile : tile + half], axis=1, keepdims=True)
+            right[m, 0:1, tile:] = right[m, 0:1, tile:] - jnp.sum(y * rows, axis=0, keepdims=True)
+            sums[m, k0 : k0 + step, :] = jnp.broadcast_to(y + noise_cols[k0 : k0 + step, m : m + 1], (step, 128))
+            low = k0 + step
+            start = low // half * half
+            if low < rank:
+                left, other = stacked3(rows[:, start - tile :])
+                change = dot_tn(left, other)
+                mats[m, low:, start:] = mats[m, low:, start:] - change[low - start :]
+
+    x = [jnp.zeros((users, 1, half), F32)] * 2
+    for k0 in range(rank - step, -1, -step):
+        t = k0 // half
+        at = pl.ds(k0, step)
+        part = mats[:, at, half:] * x[1]
+        if t == 0:
+            part = part + mats[:, at, :half] * x[0]
+        rest = sums[:, at, :] - jnp.sum(part, axis=2, keepdims=True)
+        x[t] = x[t] + jnp.sum(back[:, at, :] * rest, axis=1, keepdims=True)
     for m in range(users):
-        out[m : m + 1, :] = x[m]
+        out[m : m + 1, :half] = x[0][m]
+        out[m : m + 1, half:] = x[1][m]
 
 
 def solve_users(packed, noise, prior, shift):
@@ -342,7 +357,7 @@
         scratch_shapes=[
             pltpu.VMEM((users, rank, rank), F32),
             pltpu.VMEM((users, 8, rank), F32),
-            pltpu.VMEM((users, rank, rank), F32),
+            pltpu.VMEM((users, rank, 128), F32),
             pltpu.VMEM((users, rank, 128), F32),
         ],
         compiler_params=pltpu.CompilerParams(vmem_limit_bytes=48 * MIB),
@@ -428,13 +443,14 @@
             held[g * share : (g + 1) * share, :] = samples[d, g]
         hi, lo = split(held[...])
         other = jnp.concatenate([hi, lo, hi, lo], axis=0).astype(BF16)
+        terms = []
         for c in range(cols):
-            i = d * cols + c
-            own = jnp.where(live[i] > 0, ALPHA * weights[i], 0.0)
-            hi, lo = split(own)
+            hi, lo = split(jnp.where(live[d * cols + c] > 0, ALPHA * weights[d * cols + c], 0.0))
             left = jnp.concatenate([hi, hi, lo, lo], axis=0).astype(BF16)
-            b = listed[i]
-            out[b] = out[b] + dot_tn(left, other)
+            terms.append(dot_tn(left, other))
+        for c in range(cols):
+            b = listed[d * cols + c]
+            out[b] = out[b] + terms[c]
         return carry
 
     lax.fori_loop(0, samples.shape[0], device, 0)

time: 272 us -> 252 us (0.926)
  Pallas kernels: 177 us -> 157 us
    pallas_call x1, Pallas kernels: 56.4 us -> 36.4 us  [solve_users(): pl.pallas_call(solve_kernel, in_specs=[vmem] * 4, out_specs=vmem, out_sha...]
  transfers between devices with their start and end apart: 2 -> 2, of which waited for: 1 -> 1; matrix products, arithmetic and copies ran while one was open for 1% -> 1% of each run, Pallas kernels for 30% -> 32%
where the time goes in v4:
time: 252 us; the launch traced here: 251 us
  Pallas kernels  157 us (62%)
  waiting for transfers between devices  63.8 us (25%)
  starting transfers between devices  18.6 us (7%)
  local copies, waits for them, and re-layouts  9.71 us (4%)
    pallas_call x1, Pallas kernels, gram_terms(): pl.pallas_call(gram_kernel, in_specs=[pl.BlockSpec(memory_space=pltpu.SME...  74.6 us
    all_to_all x1, waiting for transfers between devices, on_device(): lax.all_to_all(outgoing, 'usr', split_axis=0, concat_axis=0, tiled=True)  63.8 us
    pallas_call x1, Pallas kernels, solve_users(): pl.pallas_call(solve_kernel, in_specs=[vmem] * 4, out_specs=vmem, out_sha...  36.4 us
    pallas_call x1, Pallas kernels, share_samples(): pl.pallas_call(share_kernel, in_specs=[vmem], out_specs=vmem, out_shape=j...  26.4 us
    pallas_call x1, Pallas kernels, make_stats(): pl.pallas_call(functools.partial(stats_kernel, n // peers), in_specs=[sme...  11.7 us
    all_to_all x1, starting transfers between devices, on_device(): lax.all_to_all(outgoing, 'usr', split_axis=0, concat_axis=0, tiled=True)  9.61 us
    all_to_all x1, starting transfers between devices, on_device(): lax.all_to_all(weights, 'usr', split_axis=0, concat_axis=0, tiled=True)  8.95 us
    unnamed x20, local copies, waits for them, and re-layouts  8.17 us
  transfers between devices with their start and end apart: 2, of which 1 were waited for; matrix products, arithmetic and copies ran while one was open for 1% of the time, Pallas kernels for 32%

profile of v4, /device:TPU:1, one launch (start us, length us, event | category | flops | bytes accessed | tf_op | source)
XLA Modules:
  0.0 251.4 jit_solution(1813224889583359042)
XLA Ops:
  0.6 0.0 copy-start
  0.6 0.7 fusion
  1.4 0.1 reshape.28.live
  1.5 0.8 copy.12
  2.3 0.1 reshape_squeeze.3.listed
  2.4 0.0 copy-start.3
  2.4 1.6 copy-done.3
  4.0 2.0 pick_blocks.1
  5.9 0.0 copy-start.1
  6.0 2.6 %copy-done.1 = bf16[96,128,256]{2,1,0:T(8,128)(2,1)} copy-done((bf16[96,128,256]{2,1,0:T(8,128)(2,1)}, bf16[96,128,256]{2,1,0:T(8,128)(2,1)S(1)}, u32[]{:S(2)}) %copy-start.1) | copy-done | bytes 6291480
  8.6 9.6 %all-to-all-start = ((bf16[96,128,256]{2,1,0:T(8,128)(2,1)}), bf16[96,128,256]{2,1,0:T(8,128)(2,1)}, u32[]{:S(2)}, u32[]{:S(2)}) async-start(bf16[96,128,256]{2,1,0:T(8,128)(2,1)} %copy-done.1), calls=%async_computation | async-start | bytes 12582912 | tf_op jit(solution)/shard_map/all_to_all | solution.py:486
  18.2 0.0 copy-done
  18.2 0.1 copy.14
  18.4 0.0 copy-done.5
  18.4 0.7 mul.15.refs
  19.1 0.0 copy-done.6
  19.1 6.1 %make_weights.1 = f32[96,56,128]{2,1,0:T(8,128)S(1)} custom-call(s32[56,768]{1,0:T(8,128)S(1)} %bitcast.12, bf16[56,768]{1,0:T(8,128)(2,1)S(1)} %bitcast.14), custom_call_target="tpu_custom_call" | custom-call | tf_op jit(solution)/shard_map/make_weights/pallas_call | solution.py:91
  25.2 0.0 copy-start.2
  25.2 1.5 copy-done.2
  26.7 0.7 bitcast_convert_fusion.values
  27.4 63.8 %all-to-all-done = bf16[96,128,256]{2,1,0:T(8,128)(2,1)} async-done(((bf16[96,128,256]{2,1,0:T(8,128)(2,1)}), bf16[96,128,256]{2,1,0:T(8,128)(2,1)}, u32[]{:S(2)}, u32[]{:S(2)}) %all-to-all-start) | async-done | bytes 6291488 | tf_op jit(solution)/shard_map/all_to_all | solution.py:486
  91.2 8.9 %all-to-all-start.1 = ((f32[96,56,128]{2,1,0:T(8,128)}), f32[96,56,128]{2,1,0:T(8,128)S(1)}, u32[]{:S(2)}, u32[]{:S(2)}) async-start(f32[96,56,128]{2,1,0:T(8,128)} %copy-done.2), calls=%async_computation.1 | async-start | bytes 5505024 | tf_op jit(solution)/shard_map/all_to_all | solution.py:489
  100.1 0.0 copy-start.7
  100.1 0.0 copy-start.8
  100.1 74.6 %gram_terms.1.packed = f32[14,264,128]{2,1,0:T(8,128)} custom-call(s32[43008]{0:T(1024)} %mul.15.refs, bf16[12288,256]{1,0:T(8,128)(2,1)} %bitcast.4.table, f32[56,768]{1,0:T(8,128)} %bitcast_convert_fusion.values), custom_call_target="tpu_custom_call" | custom-call | flops 60000002048 | bytes 209715200 | tf_op jit(solution)/shard_map/gram_terms/pallas_call | solution.py:233
  174.8 0.0 all-to-all-done.1.weights
  174.8 0.0 copy-done.7
  174.8 1.5 copy-done.4
  176.3 36.4 %solve_users.1.own = f32[14,256]{1,0:T(8,128)S(1)} custom-call(f32[14,264,128]{2,1,0:T(8,128)S(1)} %copy-done.4, f32[256,14]{1,0:T(8,128)S(1)} %bitcast.13, f32[256,256]{1,0:T(8,128)S(1)} %copy-done.7, f32[1,256]{1,0:T(1,128)S(1)} %bitcast.15), custom_call_target="tpu_custom_call" | custom-call | tf_op jit(solution)/shard_map/solve_users/pallas_call | solution.py:352
  212.7 26.4 %share_samples.1.samples = f32[32,4,14,256]{3,2,1,0:T(8,128)S(1)} custom-call(f32[14,256]{1,0:T(8,128)S(1)} %solve_users.1.own), custom_call_target="tpu_custom_call" | custom-call | tf_op jit(solution)/shard_map/share_samples/pallas_call | solution.py:426
  239.1 11.7 %make_stats.1 = f32[32,128,256]{2,1,0:T(8,128)} custom-call(s32[96]{0:T(128)S(1)} %reshape_squeeze.3.listed, s32[96]{0:T(128)S(1)} %reshape.28.live, f32[96,56,128]{2,1,0:T(8,128)S(1)} %all-to-all-done.1.weights, f32[32,4,14,256]{3,2,1,0:T(8,128)S(1)} %share_samples.1.samples), custom_call_target="tpu_custom_call" | custom-call | tf_op jit(solution)/shard_map/make_stats/pallas_call | solution.py:464
  250.8 0.6 reshape.27
  (7 shorter events, 0.0 us)
Async XLA Ops:
  0.6 17.6 %copy-start = (f32[56,256]{1,0:T(8,128)S(1)}, f32[56,256]{1,0:T(8,128)}, u32[]{:S(2)}) copy-start(f32[56,256]{1,0:T(8,128)} %param.13) | copy-start | bytes 172036
  2.4 1.6 copy-start.3
  5.9 2.6 %copy-start.1 = (bf16[96,128,256]{2,1,0:T(8,128)(2,1)}, bf16[96,128,256]{2,1,0:T(8,128)(2,1)S(1)}, u32[]{:S(2)}) copy-start(bf16[96,128,256]{2,1,0:T(8,128)(2,1)S(1)} %pick_blocks.1) | copy-start | bytes 18874372
  8.6 9.8 %copy-start.5 = (s32[1,56,768]{2,1,0:T(8,128)S(1)}, s32[1,56,768]{2,1,0:T(8,128)}, u32[]{:S(2)}) copy-start(s32[1,56,768]{2,1,0:T(8,128)} %param.11) | copy-start | bytes 516100
  8.6 10.5 %copy-start.6 = (bf16[1,56,768]{2,1,0:T(8,128)(2,1)S(1)}, bf16[1,56,768]{2,1,0:T(8,128)(2,1)}, u32[]{:S(2)}) copy-start(bf16[1,56,768]{2,1,0:T(8,128)(2,1)} %param.12) | copy-start | bytes 258052
  8.6 82.6 %all-to-all-start = ((bf16[96,128,256]{2,1,0:T(8,128)(2,1)}), bf16[96,128,256]{2,1,0:T(8,128)(2,1)}, u32[]{:S(2)}, u32[]{:S(2)}) async-start(bf16[96,128,256]{2,1,0:T(8,128)(2,1)} %copy-done.1), calls=%async_computation | async-start | bytes 12582912 | tf_op jit(solution)/shard_map/all_to_all | solution.py:486
  25.2 1.5 copy-start.2
  91.2 83.6 %all-to-all-start.1 = ((f32[96,56,128]{2,1,0:T(8,128)}), f32[96,56,128]{2,1,0:T(8,128)S(1)}, u32[]{:S(2)}, u32[]{:S(2)}) async-start(f32[96,56,128]{2,1,0:T(8,128)} %copy-done.2), calls=%async_computation.1 | async-start | bytes 5505024 | tf_op jit(solution)/shard_map/all_to_all | solution.py:489
  100.1 74.7 %copy-start.7 = (f32[256,256]{1,0:T(8,128)S(1)}, f32[256,256]{1,0:T(8,128)}, u32[]{:S(2)}) copy-start(f32[256,256]{1,0:T(8,128)} %prior.1) | copy-start | bytes 786436
  100.1 74.7 %copy-start.8 = (f32[256]{0:T(256)S(1)}, f32[256]{0:T(256)}, u32[]{:S(2)}) copy-start(f32[256]{0:T(256)} %param.15) | copy-start | bytes 3076
  174.8 1.5 copy-start.4

commit v5 on v4

--- a/solution.py
+++ b/solution.py
@@ -41,32 +41,39 @@
     return lax.dot_general(a, b, (((0,), (0,)), ((), ())), preferred_element_type=F32)
 
 
-def pick_kernel(cols, per_step, listed, live, blocks, out):
-    base = pl.program_id(0) * per_step
-
-    def body(i, carry):
-        keep = live[base + i] > 0
-        block = blocks[listed[base + i]]
-        out[i] = jnp.where(keep, block, jnp.zeros_like(block))
-        return carry
-
-    lax.fori_loop(0, per_step, body, 0)
+def pick_kernel(listed, live, blocks, out, zeros, sems):
+    n = out.shape[0]
+    zeros[...] = jnp.zeros_like(zeros)
+
+    def start(i, carry):
+        @pl.when(live[i] > 0)
+        def _():
+            pltpu.make_async_copy(blocks.at[listed[i]], out.at[i], sems.at[i]).start()
+
+        @pl.when(live[i] <= 0)
+        def _():
+            pltpu.make_async_copy(zeros, out.at[i], sems.at[i]).start()
+
+        return carry
+
+    def wait(i, carry):
+        pltpu.make_async_copy(zeros, out.at[i], sems.at[i]).wait()
+        return carry
+
+    lax.fori_loop(0, n, start, 0)
+    lax.fori_loop(0, n, wait, 0)
 
 
 def pick_blocks(blocks, listed, live):
     n = listed.shape[0]
     owned, height, rank = blocks.shape
-    steps = 4
-    per_step = n // steps
+    smem = pl.BlockSpec(memory_space=pltpu.SMEM)
     return pl.pallas_call(
-        functools.partial(pick_kernel, n, per_step),
-        grid_spec=pltpu.PrefetchScalarGridSpec(
-            num_scalar_prefetch=2,
-            grid=(steps,),
-            in_specs=[pl.BlockSpec((owned, height, rank), lambda s, *_: (0, 0, 0))],
-            out_specs=pl.BlockSpec((per_step, height, rank), lambda s, *_: (s, 0, 0)),
-        ),
+        pick_kernel,
+        in_specs=[smem, smem, pl.BlockSpec(memory_space=pltpu.HBM)],
+        out_specs=pl.BlockSpec(memory_space=pltpu.HBM),
         out_shape=jax.ShapeDtypeStruct((n, height, rank), BF16),
+        scratch_shapes=[pltpu.VMEM((height, rank), BF16), pltpu.SemaphoreType.DMA((n,))],
         compiler_params=pltpu.CompilerParams(vmem_limit_bytes=32 * MIB),
         name="pick_blocks",
     )(listed, live, blocks)
@@ -127,16 +134,45 @@
     store(256, jnp.where(row == 0, diag, tail))
 
 
-def gram_kernel(refs, table, values, out, wide, even, odd, stage, near, far, send_sem, recv_sem):
+def gram_kernel(
+    refs, table, values, weights, out, gathered, wide, even, odd, stage, near, far, send_sem, recv_sem, give_sem, take_sem, own_sem
+):
     rows = table.shape[0]
     share, height, _ = out.shape
     chunk, cut = 128, near.shape[2] // 16 * 8
     me, ring = lax.axis_index("grp"), 4
     after, before = (me + 1) % ring, (me + ring - 1) % ring
+    u, peers = lax.axis_index("usr"), lax.axis_size("usr")
+    cols = weights.shape[0] // peers
 
     barrier = pltpu.get_barrier_semaphore()
     for peer in (after, before):
         pl.semaphore_signal(barrier, inc=1, device_id={"grp": peer}, device_id_type=MESH)
+    for o in range(1, peers):
+        pl.semaphore_signal(barrier, inc=1, device_id={"usr": (u + o) % peers}, device_id_type=MESH)
+
+    def give(o):
+        peer = (u + o) % peers
+        return pltpu.make_async_remote_copy(
+            src_ref=weights.at[pl.ds(peer * cols, cols)],
+            dst_ref=gathered.at[pl.ds(u * cols, cols)],
+            send_sem=give_sem.at[o],
+            recv_sem=take_sem.at[o],
+            device_id={"usr": peer},
+            device_id_type=MESH,
+        )
+
+    def take(o):
+        peer = (u + peers - o) % peers
+        slab = gathered.at[pl.ds(peer * cols, cols)]
+        return pltpu.make_async_remote_copy(
+            src_ref=slab,
+            dst_ref=slab,
+            send_sem=give_sem.at[o],
+            recv_sem=take_sem.at[o],
+            device_id={"usr": peer},
+            device_id_type=MESH,
+        )
 
     def widen(i, carry):
         part = table[pl.ds(i * chunk, chunk), :].astype(F32)
@@ -145,7 +181,18 @@
         return carry
 
     lax.fori_loop(0, rows // chunk, widen, 0)
-    pl.semaphore_wait(barrier, 2)
+    pl.semaphore_wait(barrier, peers + 1)
+
+    keep = pltpu.make_async_copy(
+        weights.at[pl.ds(u * cols, cols)], gathered.at[pl.ds(u * cols, cols)], own_sem
+    )
+    keep.start()
+
+    def send_weights(o, carry):
+        give(o).start()
+        return carry
+
+    lax.fori_loop(1, peers, send_weights, 0)
 
     def copy(j, kind):
         if kind == 0:
@@ -223,18 +270,31 @@
 
     lax.fori_loop(0, share, drain, 0)
 
-
-def gram_terms(table, refs, values):
+    def drain_weights(o, carry):
+        give(o).wait_send()
+        take(o).wait_recv()
+        return carry
+
+    lax.fori_loop(1, peers, drain_weights, 0)
+    keep.wait()
+
+
+def gram_terms(table, refs, values, weights):
     users, slots = refs.shape
     rows, rank = table.shape
     ring, height = 4, 264
     share = users // ring
+    peers = lax.axis_size("usr")
     vmem = pl.BlockSpec(memory_space=pltpu.VMEM)
+    hbm = pl.BlockSpec(memory_space=pltpu.HBM)
     return pl.pallas_call(
         gram_kernel,
-        in_specs=[pl.BlockSpec(memory_space=pltpu.SMEM), vmem, vmem],
-        out_specs=vmem,
-        out_shape=jax.ShapeDtypeStruct((share, height, 128), F32),
+        in_specs=[pl.BlockSpec(memory_space=pltpu.SMEM), vmem, vmem, hbm],
+        out_specs=(vmem, hbm),
+        out_shape=(
+            jax.ShapeDtypeStruct((share, height, 128), F32),
+            jax.ShapeDtypeStruct(weights.shape, F32),
+        ),
         scratch_shapes=[
             pltpu.VMEM((2 * rows, 128), F32),
             pltpu.VMEM((2 * slots, 128), F32),
@@ -244,11 +304,14 @@
             pltpu.VMEM((2, share, height, 128), F32),
             pltpu.SemaphoreType.DMA((share, 4)),
             pltpu.SemaphoreType.DMA((share, 4)),
+            pltpu.SemaphoreType.DMA((peers,)),
+            pltpu.SemaphoreType.DMA((peers,)),
+            pltpu.SemaphoreType.DMA(()),
         ],
         compiler_params=pltpu.CompilerParams(vmem_limit_bytes=56 * MIB, collective_id=0, has_side_effects=True),
         cost_estimate=pl.CostEstimate(flops=60 * 10**9, bytes_accessed=200 * MIB, transcendentals=0),
         name="gram_terms",
-    )((2 * refs).reshape(users * slots), table, values.astype(F32))
+    )((2 * refs).reshape(users * slots), table, values.astype(F32), weights)
 
 
 def solve_kernel(packed, noise_cols, prior, shift, out, mats, right, back, sums):
@@ -275,19 +338,42 @@
     lane = iota((1, 8, 128), 2)
     tall_lane = iota((step, 128), 1)
 
+    flat_lane = iota((8, 128), 1)
+
     def column(x, k):
-        return jnp.broadcast_to(x[:, :, k : k + 1], x.shape)
-
+        at = flat_lane // (2 * step) * (2 * step) + k
+        return jnp.stack([jnp.take_along_axis(x[p], at, axis=1) for p in range(users // 2)])
+
+    def later_work(m, k0, turn, rows, left, other):
+        tile, group = k0 // half * half, k0 % half // step
+        if not group:
+            turn = pltpu.roll(turn, half - step, 1)
+        keep = (tall_lane >= group * step) & (tall_lane < (group + 1) * step)
+        turn = jnp.where(keep, turn, 0.0)
+        back[m, k0 : k0 + step, :] = turn
+        y = jnp.sum(turn * right[m, 0:1, tile : tile + half], axis=1, keepdims=True)
+        right[m, 0:1, tile:] = right[m, 0:1, tile:] - jnp.sum(y * rows, axis=0, keepdims=True)
+        sums[m, k0 : k0 + step, :] = jnp.broadcast_to(y + noise_cols[k0 : k0 + step, m : m + 1], (step, 128))
+        low = k0 + 2 * step
+        if low < rank:
+            start = low // half * half
+            change = dot_tn(left[:, start - tile :], other[:, start - tile :])
+            mats[m, low:, start:] = mats[m, low:, start:] - change[low - start :]
+
+    waiting = []
     for k0 in range(0, rank, step):
         tile, group = k0 // half * half, k0 % half // step
         parts, pivots = [], []
         for h in range(step // 8):
             rows = mats[:, k0 + 8 * h : k0 + 8 * h + 8, tile : tile + half]
-            if group:
-                rows = jnp.stack([pltpu.roll(rows[m], half - group * step, 1) for m in range(users)])
+            both = []
+            for m in range(0, users, 2):
+                turns = [(half - group * step) % half, (half + 2 * step - group * step) % half]
+                one, two = [pltpu.roll(rows[m + e], turns[e], 1) if turns[e] else rows[m + e] for e in range(2)]
+                both.append(jnp.where(lane[0] < 2 * step, one, two))
             unit = jnp.where(lane % step == sub + 8 * h, 1.0, 0.0)
-            parts.append(jnp.where(lane < step, rows, unit))
-            pivots.append(jnp.ones((users, 8, 128), F32))
+            parts.append(jnp.where(lane % (2 * step) < step, jnp.stack(both), unit))
+            pivots.append(jnp.ones((users // 2, 8, 128), F32))
         for k in range(0, step, 2):
             f, kk = k // 8, k % 8
             ones = [column(parts[h], k) for h in range(f, step // 8)]
@@ -305,9 +391,17 @@
                 if h == f:
                     new = jnp.where(sub > kk + 1, new, jnp.where(sub == kk + 1, second_row, parts[h]))
                 parts[h] = new
+            if waiting:
+                later_work(*waiting.pop(0))
+        while waiting:
+            later_work(*waiting.pop(0))
         scaled = [p * lax.rsqrt(v) for p, v in zip(parts, pivots)]
         for m in range(users):
-            turn = jnp.concatenate([x[m] for x in scaled], axis=0)
+            turn = jnp.concatenate([x[m // 2] for x in scaled], axis=0)
+            at = (m % 2) * 2 * step + step
+            turn = jnp.where((tall_lane >= at) & (tall_lane < at + step), turn, 0.0)
+            ways = (step, 2 * step) if m % 2 == 0 else (2 * step, 3 * step)
+            turn = turn + pltpu.roll(turn, ways[0], 1) + pltpu.roll(turn, ways[1], 1)
             hi, mid, low = split3(turn)
             one = jnp.where(tall_lane < step, 0.0, jnp.where(tall_lane < 3 * step, hi, mid))
             two = jnp.where(tall_lane < step, 0.0, jnp.where(tall_lane < 2 * step, hi, jnp.where(tall_lane < 3 * step, low, mid)))
@@ -316,20 +410,16 @@
             other = jnp.concatenate([hi, hi, mid, hi, hi, low, hi, mid], axis=0).astype(BF16)
             rows = jnp.dot(left, other, preferred_element_type=F32)
             mats[m, k0 : k0 + step, tile:] = rows
-            if not group:
-                turn = pltpu.roll(turn, half - step, 1)
-            keep = (tall_lane >= group * step) & (tall_lane < (group + 1) * step)
-            turn = jnp.where(keep, turn, 0.0)
-            back[m, k0 : k0 + step, :] = turn
-            y = jnp.sum(turn * right[m, 0:1, tile : tile + half], axis=1, keepdims=True)
-            right[m, 0:1, tile:] = right[m, 0:1, tile:] - jnp.sum(y * rows, axis=0, keepdims=True)
-            sums[m, k0 : k0 + step, :] = jnp.broadcast_to(y + noise_cols[k0 : k0 + step, m : m + 1], (step, 128))
-            low = k0 + step
-            start = low // half * half
-            if low < rank:
-                left, other = stacked3(rows[:, start - tile :])
-                change = dot_tn(left, other)
-                mats[m, low:, start:] = mats[m, low:, start:] - change[low - start :]
+            near = k0 + step
+            left, other = stacked3(rows)
+            if near < rank:
+                start = near // half * half
+                change = dot_tn(left[:, start - tile : start - tile + half], other[:, start - tile :])
+                change = change[near - start : near - start + step]
+                mats[m, near : near + step, start:] = mats[m, near : near + step, start:] - change
+            waiting.append((m, k0, turn, rows, left, other))
+    while waiting:
+        later_work(*waiting.pop(0))
 
     x = [jnp.zeros((users, 1, half), F32)] * 2
     for k0 in range(rank - step, -1, -step):
@@ -437,23 +527,28 @@
 def stats_kernel(cols, listed, live, weights, samples, out, held):
     out[...] = jnp.zeros_like(out)
     parts, share = samples.shape[1:3]
-
-    def device(d, carry):
+    unroll = 4
+
+    def device(d):
         for g in range(parts):
             held[g * share : (g + 1) * share, :] = samples[d, g]
         hi, lo = split(held[...])
-        other = jnp.concatenate([hi, lo, hi, lo], axis=0).astype(BF16)
+        other = jnp.concatenate([hi, lo, hi], axis=0).astype(BF16)
         terms = []
         for c in range(cols):
             hi, lo = split(jnp.where(live[d * cols + c] > 0, ALPHA * weights[d * cols + c], 0.0))
-            left = jnp.concatenate([hi, hi, lo, lo], axis=0).astype(BF16)
+            left = jnp.concatenate([hi, hi, lo], axis=0).astype(BF16)
             terms.append(dot_tn(left, other))
         for c in range(cols):
             b = listed[d * cols + c]
             out[b] = out[b] + terms[c]
-        return carry
-
-    lax.fori_loop(0, samples.shape[0], device, 0)
+
+    def devices(i, carry):
+        for e in range(unroll):
+            device(unroll * i + e)
+        return carry
+
+    lax.fori_loop(0, samples.shape[0] // unroll, devices, 0)
 
 
 def make_stats(weights, samples, listed, live, owned):
@@ -485,11 +580,7 @@
     outgoing = pick_blocks(blocks, listed, live)
     incoming = lax.all_to_all(outgoing, "usr", split_axis=0, concat_axis=0, tiled=True)
     weights = make_weights(refs, values, n, height)
-    incoming, weights = lax.optimization_barrier((incoming, weights))
-    gathered = lax.all_to_all(weights, "usr", split_axis=0, concat_axis=0, tiled=True)
-
-    packed = gram_terms(incoming.reshape(n * height, rank), refs, values)
-    packed, gathered = lax.optimization_barrier((packed, gathered))
+    packed, gathered = gram_terms(incoming.reshape(n * height, rank), refs, values, weights)
     share = packed.shape[0]
     draws = lax.dynamic_slice_in_dim(noise, lax.axis_index("grp") * share, share, 0)
     everyone = share_samples(solve_users(packed, draws, prior_prec, prior_shift))

time: 252 us -> 246 us (0.976)
  starting transfers between devices: 18.6 us -> 9.63 us
    pallas_call x1, Pallas kernels: 1.97 us -> 12.1 us  [pick_blocks(): pl.pallas_call(pick_kernel, in_specs=[smem, smem, pl.BlockSpec(memory_spa...]
    all_to_all x1 -> x0, starting transfers between devices: 8.95 us -> none  [on_device(): lax.all_to_all(weights, 'usr', split_axis=0, concat_axis=0, tiled=True)]
    pallas_call x1, Pallas kernels: 36.4 us -> 28.2 us  [solve_users(): pl.pallas_call(solve_kernel, in_specs=[vmem] * 4, out_specs=vmem, out_sha...]
    pallas_call x1, Pallas kernels: 74.6 us -> 81 us  [gram_terms(): pl.pallas_call(gram_kernel, in_specs=[pl.BlockSpec(memory_space=pltpu.SME...]
    pallas_call x1, Pallas kernels: 11.7 us -> 6.3 us  [make_stats(): pl.pallas_call(functools.partial(stats_kernel, n // peers), in_specs=[sme...]
    unnamed x20 -> x22, local copies, waits for them, and re-layouts: 8.17 us -> 9.96 us
  transfers between devices with their start and end apart: 2 -> 1, of which waited for: 1 -> 1; matrix products, arithmetic and copies ran while one was open for 1% -> 1% of each run, Pallas kernels for 32% -> 2%
where the time goes in v5:
time: 246 us
  Pallas kernels  159 us (65%)
  waiting for transfers between devices  63.8 us (26%)
  local copies, waits for them, and re-layouts  11.5 us (5%)
  starting transfers between devices  9.63 us (4%)
    pallas_call x1, Pallas kernels, gram_terms(): pl.pallas_call(gram_kernel, in_specs=[pl.BlockSpec(memory_space=pltpu.SME...  81 us
    all_to_all x1, waiting for transfers between devices, on_device(): lax.all_to_all(outgoing, 'usr', split_axis=0, concat_axis=0, tiled=True)  63.8 us
    pallas_call x1, Pallas kernels, solve_users(): pl.pallas_call(solve_kernel, in_specs=[vmem] * 4, out_specs=vmem, out_sha...  28.2 us
    pallas_call x1, Pallas kernels, share_samples(): pl.pallas_call(share_kernel, in_specs=[vmem], out_specs=vmem, out_shape=j...  24.9 us
    pallas_call x1, Pallas kernels, pick_blocks(): pl.pallas_call(pick_kernel, in_specs=[smem, smem, pl.BlockSpec(memory_spa...  12.1 us
    unnamed x22, local copies, waits for them, and re-layouts  9.96 us
    all_to_all x1, starting transfers between devices, on_device(): lax.all_to_all(outgoing, 'usr', split_axis=0, concat_axis=0, tiled=True)  9.63 us
    pallas_call x1, Pallas kernels, make_stats(): pl.pallas_call(functools.partial(stats_kernel, n // peers), in_specs=[sme...  6.3 us
  transfers between devices with their start and end apart: 1, of which 1 were waited for; matrix products, arithmetic and copies ran while one was open for 1% of the time, Pallas kernels for 2%

profile of v5, /device:TPU:1, one launch (start us, length us, event | category | flops | bytes accessed | tf_op | source)
XLA Modules:
  0.0 245.7 jit_solution(13827187741232214685)
XLA Ops:
  0.6 0.0 copy-start
  0.6 0.8 copy.12
  1.4 0.1 reshape_squeeze.3.listed
  1.5 0.7 fusion
  2.3 0.1 reshape.28.live
  2.4 0.0 copy-start.4
  2.4 1.6 copy-done.4
  4.0 12.1 %pick_blocks.1 = bf16[96,128,256]{2,1,0:T(8,128)(2,1)S(1)} custom-call(s32[96]{0:T(128)S(1)} %reshape_squeeze.3.listed, s32[96]{0:T(128)S(1)} %reshape.28.live, bf16[32,128,256]{2,1,0:T(8,128)(2,1)S(1)} %bitcast.11), custom_call_target="tpu_custom_call" | custom-call | tf_op jit(solution)/shard_map/pick_blocks/pallas_call | solution.py:71
  16.1 0.0 copy-start.1
  16.1 2.6 %copy-done.1 = bf16[96,128,256]{2,1,0:T(8,128)(2,1)} copy-done((bf16[96,128,256]{2,1,0:T(8,128)(2,1)}, bf16[96,128,256]{2,1,0:T(8,128)(2,1)S(1)}, u32[]{:S(2)}) %copy-start.1) | copy-done | bytes 6291480
  18.7 0.0 copy-start.7
  18.7 9.6 %all-to-all-start = ((bf16[96,128,256]{2,1,0:T(8,128)(2,1)}), bf16[96,128,256]{2,1,0:T(8,128)(2,1)}, u32[]{:S(2)}, u32[]{:S(2)}) async-start(bf16[96,128,256]{2,1,0:T(8,128)(2,1)} %copy-done.1), calls=%async_computation | async-start | bytes 12582912 | tf_op jit(solution)/shard_map/all_to_all | solution.py:581
  28.4 0.0 copy-done.6
  28.4 0.7 mul.15.refs
  29.1 0.0 copy-done
  29.1 0.1 copy.14
  29.2 0.0 copy-done.7
  29.2 6.1 %make_weights.1.weights = f32[96,56,128]{2,1,0:T(8,128)S(1)} custom-call(s32[56,768]{1,0:T(8,128)S(1)} %bitcast.12, bf16[56,768]{1,0:T(8,128)(2,1)S(1)} %bitcast.14), custom_call_target="tpu_custom_call" | custom-call | tf_op jit(solution)/shard_map/make_weights/pallas_call | solution.py:98
  35.3 0.0 copy-start.3
  35.3 1.5 copy-done.3
  36.9 0.7 bitcast_convert_fusion.values
  37.5 63.8 %all-to-all-done = bf16[96,128,256]{2,1,0:T(8,128)(2,1)} async-done(((bf16[96,128,256]{2,1,0:T(8,128)(2,1)}), bf16[96,128,256]{2,1,0:T(8,128)(2,1)}, u32[]{:S(2)}, u32[]{:S(2)}) %all-to-all-start) | async-done | bytes 6291488 | tf_op jit(solution)/shard_map/all_to_all | solution.py:581
  101.3 81.0 %gram_terms.1 = (f32[14,264,128]{2,1,0:T(8,128)}, f32[96,56,128]{2,1,0:T(8,128)}) custom-call(s32[43008]{0:T(1024)} %mul.15.refs, bf16[12288,256]{1,0:T(8,128)(2,1)} %bitcast.2.table, f32[56,768]{1,0:T(8,128)} %bitcast_convert_fusion.values, f32[96,56,128]{2,1,0:T(8,128)} %copy-done.3), custom_call_target="tpu_custom_call" | custom-call | flops 60000002048 | bytes 209715200 | tf_op jit(solution)/shard_map/gram_terms/pallas_call | solution.py:290
  182.3 0.0 copy-done.8
  182.3 0.0 copy-done.9
  182.4 0.0 copy-start.5
  182.4 1.5 copy-done.5
  183.9 28.2 %solve_users.1.own = f32[14,256]{1,0:T(8,128)S(1)} custom-call(f32[14,264,128]{2,1,0:T(8,128)S(1)} %copy-done.5, f32[256,14]{1,0:T(8,128)S(1)} %bitcast.13, f32[256,256]{1,0:T(8,128)S(1)} %copy-done.8, f32[1,256]{1,0:T(1,128)S(1)} %bitcast.15), custom_call_target="tpu_custom_call" | custom-call | tf_op jit(solution)/shard_map/solve_users/pallas_call | solution.py:442
  212.1 24.9 %share_samples.1.samples = f32[32,4,14,256]{3,2,1,0:T(8,128)S(1)} custom-call(f32[14,256]{1,0:T(8,128)S(1)} %solve_users.1.own), custom_call_target="tpu_custom_call" | custom-call | tf_op jit(solution)/shard_map/share_samples/pallas_call | solution.py:516
  237.0 0.6 reshape.27
  237.7 1.8 copy-done.2
  239.4 6.3 %make_stats.1 = f32[32,128,256]{2,1,0:T(8,128)} custom-call(s32[96]{0:T(128)S(1)} %reshape_squeeze.3.listed, s32[96]{0:T(128)S(1)} %reshape.28.live, f32[96,56,128]{2,1,0:T(8,128)S(1)} %copy-done.2, f32[32,4,14,256]{3,2,1,0:T(8,128)S(1)} %share_samples.1.samples), custom_call_target="tpu_custom_call" | custom-call | tf_op jit(solution)/shard_map/make_stats/pallas_call | solution.py:559
  (7 shorter events, 0.0 us)
Async XLA Ops:
  0.6 28.5 %copy-start = (f32[56,256]{1,0:T(8,128)S(1)}, f32[56,256]{1,0:T(8,128)}, u32[]{:S(2)}) copy-start(f32[56,256]{1,0:T(8,128)} %param.13) | copy-start | bytes 172036
  2.4 1.6 copy-start.4
  16.1 2.6 %copy-start.1 = (bf16[96,128,256]{2,1,0:T(8,128)(2,1)}, bf16[96,128,256]{2,1,0:T(8,128)(2,1)S(1)}, u32[]{:S(2)}) copy-start(bf16[96,128,256]{2,1,0:T(8,128)(2,1)S(1)} %pick_blocks.1) | copy-start | bytes 18874372
  18.7 9.7 %copy-start.6 = (s32[1,56,768]{2,1,0:T(8,128)S(1)}, s32[1,56,768]{2,1,0:T(8,128)}, u32[]{:S(2)}) copy-start(s32[1,56,768]{2,1,0:T(8,128)} %param.11) | copy-start | bytes 516100
  18.7 10.5 %copy-start.7 = (bf16[1,56,768]{2,1,0:T(8,128)(2,1)S(1)}, bf16[1,56,768]{2,1,0:T(8,128)(2,1)}, u32[]{:S(2)}) copy-start(bf16[1,56,768]{2,1,0:T(8,128)(2,1)} %param.12) | copy-start | bytes 258052
  18.7 82.6 %all-to-all-start = ((bf16[96,128,256]{2,1,0:T(8,128)(2,1)}), bf16[96,128,256]{2,1,0:T(8,128)(2,1)}, u32[]{:S(2)}, u32[]{:S(2)}) async-start(bf16[96,128,256]{2,1,0:T(8,128)(2,1)} %copy-done.1), calls=%async_computation | async-start | bytes 12582912 | tf_op jit(solution)/shard_map/all_to_all | solution.py:581
  35.3 1.5 copy-start.3
  101.3 81.0 %copy-start.8 = (f32[256,256]{1,0:T(8,128)S(1)}, f32[256,256]{1,0:T(8,128)}, u32[]{:S(2)}) copy-start(f32[256,256]{1,0:T(8,128)} %prior.1) | copy-start | bytes 786436
  101.3 81.0 %copy-start.9 = (f32[256]{0:T(256)S(1)}, f32[256]{0:T(256)}, u32[]{:S(2)}) copy-start(f32[256]{0:T(256)} %param.15) | copy-start | bytes 3076
  182.4 1.5 copy-start.5
  237.7 1.8 copy-start.2

commit v6 on v5

--- a/solution.py
+++ b/solution.py
@@ -41,39 +41,32 @@
     return lax.dot_general(a, b, (((0,), (0,)), ((), ())), preferred_element_type=F32)
 
 
-def pick_kernel(listed, live, blocks, out, zeros, sems):
-    n = out.shape[0]
-    zeros[...] = jnp.zeros_like(zeros)
-
-    def start(i, carry):
-        @pl.when(live[i] > 0)
-        def _():
-            pltpu.make_async_copy(blocks.at[listed[i]], out.at[i], sems.at[i]).start()
-
-        @pl.when(live[i] <= 0)
-        def _():
-            pltpu.make_async_copy(zeros, out.at[i], sems.at[i]).start()
-
-        return carry
-
-    def wait(i, carry):
-        pltpu.make_async_copy(zeros, out.at[i], sems.at[i]).wait()
-        return carry
-
-    lax.fori_loop(0, n, start, 0)
-    lax.fori_loop(0, n, wait, 0)
+def pick_kernel(cols, per_step, listed, live, blocks, out):
+    base = pl.program_id(0) * per_step
+
+    def body(i, carry):
+        keep = live[base + i] > 0
+        block = blocks[listed[base + i]]
+        out[i] = jnp.where(keep, block, jnp.zeros_like(block))
+        return carry
+
+    lax.fori_loop(0, per_step, body, 0)
 
 
 def pick_blocks(blocks, listed, live):
     n = listed.shape[0]
     owned, height, rank = blocks.shape
-    smem = pl.BlockSpec(memory_space=pltpu.SMEM)
+    steps = 4
+    per_step = n // steps
     return pl.pallas_call(
-        pick_kernel,
-        in_specs=[smem, smem, pl.BlockSpec(memory_space=pltpu.HBM)],
-        out_specs=pl.BlockSpec(memory_space=pltpu.HBM),
+        functools.partial(pick_kernel, n, per_step),
+        grid_spec=pltpu.PrefetchScalarGridSpec(
+            num_scalar_prefetch=2,
+            grid=(steps,),
+            in_specs=[pl.BlockSpec((owned, height, rank), lambda s, *_: (0, 0, 0))],
+            out_specs=pl.BlockSpec((per_step, height, rank), lambda s, *_: (s, 0, 0)),
+        ),
         out_shape=jax.ShapeDtypeStruct((n, height, rank), BF16),
-        scratch_shapes=[pltpu.VMEM((height, rank), BF16), pltpu.SemaphoreType.DMA((n,))],
         compiler_params=pltpu.CompilerParams(vmem_limit_bytes=32 * MIB),
         name="pick_blocks",
     )(listed, live, blocks)
@@ -236,32 +229,45 @@
 
     gather_rows(wide, even, refs, user(0, 2))
 
-    def turn(j, carry):
-        gather_rows(wide, odd, refs, user(j, 1))
-        terms(even, j, 2)
-        copy(j, 0).start()
-        copy(j, 1).start()
-        gather_rows(wide, even, refs, user(j, 3))
-        terms(odd, j, 1)
-        gather_rows(wide, odd, refs, user(j, 0))
-        terms(even, j, 3)
-        gather_rows(wide, even, refs, user((j + 1) % share, 2))
-        terms(odd, j, 0)
-
-        @pl.when(j >= 1)
-        def _():
-            pass_on(j - 1)
-
-        @pl.when(j >= 2)
-        def _():
-            finish(j - 2)
-
-        return carry
-
-    lax.fori_loop(0, share, turn, 0)
-    pass_on(share - 1)
-    finish(share - 2)
-    finish(share - 1)
+    def furthest(i, carry):
+        gather_rows(wide, odd, refs, user(2 * i + 1, 2))
+        terms(even, 2 * i, 2)
+        copy(2 * i, 0).start()
+        copy(2 * i, 1).start()
+        following = 2 * i + 2
+        gather_rows(wide, even, refs, user(following % share, 2 - following // share))
+        terms(odd, 2 * i + 1, 2)
+        copy(2 * i + 1, 0).start()
+        copy(2 * i + 1, 1).start()
+        return carry
+
+    lax.fori_loop(0, share // 2, furthest, 0)
+
+    def neighbours(j, carry):
+        gather_rows(wide, odd, refs, user(j, 3))
+        terms(even, j, 1)
+        following = j + 1
+        gather_rows(wide, even, refs, user(following % share, 1 - following // share))
+        terms(odd, j, 3)
+        pass_on(j)
+        return carry
+
+    lax.fori_loop(0, share, neighbours, 0)
+
+    def own_terms(i, carry):
+        gather_rows(wide, odd, refs, user(2 * i + 1, 0))
+        terms(even, 2 * i, 0)
+        gather_rows(wide, even, refs, user((2 * i + 2) % share, 0))
+        terms(odd, 2 * i + 1, 0)
+        return carry
+
+    lax.fori_loop(0, share // 2, own_terms, 0)
+
+    def finish_all(j, carry):
+        finish(j)
+        return carry
+
+    lax.fori_loop(0, share, finish_all, 0)
 
     def drain(j, carry):
         for kind in range(4):

time: 246 us -> 234 us (0.951)
  Pallas kernels: 159 us -> 147 us
    pallas_call x1, Pallas kernels: 12.1 us -> 1.97 us  [pick_blocks(): pl.pallas_call(functools.partial(pick_kernel, n, per_step), grid_spec=plt...]
    pallas_call x1, Pallas kernels: 81 us -> 78.3 us  [gram_terms(): pl.pallas_call(gram_kernel, in_specs=[pl.BlockSpec(memory_space=pltpu.SME...]
  transfers between devices with their start and end apart: 1 -> 1, of which waited for: 1 -> 1; matrix products, arithmetic and copies ran while one was open for 1% -> 1% of each run, Pallas kernels for 2% -> 3%
where the time goes in v6:
time: 234 us
  Pallas kernels  147 us (63%)
  waiting for transfers between devices  63.8 us (27%)
  local copies, waits for them, and re-layouts  11.5 us (5%)
  starting transfers between devices  9.61 us (4%)
    pallas_call x1, Pallas kernels, gram_terms(): pl.pallas_call(gram_kernel, in_specs=[pl.BlockSpec(memory_space=pltpu.SME...  78.3 us
    all_to_all x1, waiting for transfers between devices, on_device(): lax.all_to_all(outgoing, 'usr', split_axis=0, concat_axis=0, tiled=True)  63.8 us
    pallas_call x1, Pallas kernels, solve_users(): pl.pallas_call(solve_kernel, in_specs=[vmem] * 4, out_specs=vmem, out_sha...  28.2 us
    pallas_call x1, Pallas kernels, share_samples(): pl.pallas_call(share_kernel, in_specs=[vmem], out_specs=vmem, out_shape=j...  26.2 us
    unnamed x22, local copies, waits for them, and re-layouts  9.96 us
    all_to_all x1, starting transfers between devices, on_device(): lax.all_to_all(outgoing, 'usr', split_axis=0, concat_axis=0, tiled=True)  9.61 us
    pallas_call x1, Pallas kernels, make_stats(): pl.pallas_call(functools.partial(stats_kernel, n // peers), in_specs=[sme...  6.3 us
    pallas_call x1, Pallas kernels, make_weights(): pl.pallas_call(weight_kernel, grid=(users // group,), in_specs=[pl.BlockS...  6.1 us
  transfers between devices with their start and end apart: 1, of which 1 were waited for; matrix products, arithmetic and copies ran while one was open for 1% of the time, Pallas kernels for 3%

profile of v6, /device:TPU:1, one launch (start us, length us, event | category | flops | bytes accessed | tf_op | source)
XLA Modules:
  0.0 234.1 jit_solution(9463698728743461320)
XLA Ops:
  0.6 0.0 copy-start
  0.6 0.8 copy.12
  1.4 0.1 reshape_squeeze.3.listed
  1.5 0.7 fusion
  2.3 0.1 reshape.28.live
  2.4 0.0 copy-start.4
  2.4 1.6 copy-done.4
  4.0 2.0 pick_blocks.1
  5.9 0.0 copy-start.1
  6.0 2.6 %copy-done.1 = bf16[96,128,256]{2,1,0:T(8,128)(2,1)} copy-done((bf16[96,128,256]{2,1,0:T(8,128)(2,1)}, bf16[96,128,256]{2,1,0:T(8,128)(2,1)S(1)}, u32[]{:S(2)}) %copy-start.1) | copy-done | bytes 6291480
  8.6 0.0 copy-start.6
  8.6 9.6 %all-to-all-start = ((bf16[96,128,256]{2,1,0:T(8,128)(2,1)}), bf16[96,128,256]{2,1,0:T(8,128)(2,1)}, u32[]{:S(2)}, u32[]{:S(2)}) async-start(bf16[96,128,256]{2,1,0:T(8,128)(2,1)} %copy-done.1), calls=%async_computation | async-start | bytes 12582912 | tf_op jit(solution)/shard_map/all_to_all | solution.py:587
  18.2 0.0 copy-done.6
  18.2 0.7 mul.15.refs
  18.9 0.0 copy-done
  18.9 0.1 copy.14
  19.1 0.0 copy-done.7
  19.1 6.1 %make_weights.1.weights = f32[96,56,128]{2,1,0:T(8,128)S(1)} custom-call(s32[56,768]{1,0:T(8,128)S(1)} %bitcast.12, bf16[56,768]{1,0:T(8,128)(2,1)S(1)} %bitcast.14), custom_call_target="tpu_custom_call" | custom-call | tf_op jit(solution)/shard_map/make_weights/pallas_call | solution.py:91
  25.2 0.0 copy-start.3
  25.2 1.5 copy-done.3
  26.7 0.7 bitcast_convert_fusion.values
  27.4 63.8 %all-to-all-done = bf16[96,128,256]{2,1,0:T(8,128)(2,1)} async-done(((bf16[96,128,256]{2,1,0:T(8,128)(2,1)}), bf16[96,128,256]{2,1,0:T(8,128)(2,1)}, u32[]{:S(2)}, u32[]{:S(2)}) %all-to-all-start) | async-done | bytes 6291488 | tf_op jit(solution)/shard_map/all_to_all | solution.py:587
  91.2 78.3 %gram_terms.1 = (f32[14,264,128]{2,1,0:T(8,128)}, f32[96,56,128]{2,1,0:T(8,128)}) custom-call(s32[43008]{0:T(1024)} %mul.15.refs, bf16[12288,256]{1,0:T(8,128)(2,1)} %bitcast.2.table, f32[56,768]{1,0:T(8,128)} %bitcast_convert_fusion.values, f32[96,56,128]{2,1,0:T(8,128)} %copy-done.3), custom_call_target="tpu_custom_call" | custom-call | flops 60000002048 | bytes 209715200 | tf_op jit(solution)/shard_map/gram_terms/pallas_call | solution.py:296
  169.5 0.0 copy-done.8
  169.5 0.0 copy-done.9
  169.5 0.0 copy-start.5
  169.5 1.5 copy-done.5
  171.0 28.2 %solve_users.1.own = f32[14,256]{1,0:T(8,128)S(1)} custom-call(f32[14,264,128]{2,1,0:T(8,128)S(1)} %copy-done.5, f32[256,14]{1,0:T(8,128)S(1)} %bitcast.13, f32[256,256]{1,0:T(8,128)S(1)} %copy-done.8, f32[1,256]{1,0:T(1,128)S(1)} %bitcast.15), custom_call_target="tpu_custom_call" | custom-call | tf_op jit(solution)/shard_map/solve_users/pallas_call | solution.py:448
  199.2 26.2 %share_samples.1.samples = f32[32,4,14,256]{3,2,1,0:T(8,128)S(1)} custom-call(f32[14,256]{1,0:T(8,128)S(1)} %solve_users.1.own), custom_call_target="tpu_custom_call" | custom-call | tf_op jit(solution)/shard_map/share_samples/pallas_call | solution.py:522
  225.4 0.6 reshape.27
  226.0 1.8 copy-done.2
  227.8 6.3 %make_stats.1 = f32[32,128,256]{2,1,0:T(8,128)} custom-call(s32[96]{0:T(128)S(1)} %reshape_squeeze.3.listed, s32[96]{0:T(128)S(1)} %reshape.28.live, f32[96,56,128]{2,1,0:T(8,128)S(1)} %copy-done.2, f32[32,4,14,256]{3,2,1,0:T(8,128)S(1)} %share_samples.1.samples), custom_call_target="tpu_custom_call" | custom-call | tf_op jit(solution)/shard_map/make_stats/pallas_call | solution.py:565
  (7 shorter events, 0.0 us)
Async XLA Ops:
  0.6 18.3 %copy-start = (f32[56,256]{1,0:T(8,128)S(1)}, f32[56,256]{1,0:T(8,128)}, u32[]{:S(2)}) copy-start(f32[56,256]{1,0:T(8,128)} %param.13) | copy-start | bytes 172036
  2.4 1.6 copy-start.4
  5.9 2.6 %copy-start.1 = (bf16[96,128,256]{2,1,0:T(8,128)(2,1)}, bf16[96,128,256]{2,1,0:T(8,128)(2,1)S(1)}, u32[]{:S(2)}) copy-start(bf16[96,128,256]{2,1,0:T(8,128)(2,1)S(1)} %pick_blocks.1) | copy-start | bytes 18874372
  8.6 9.6 %copy-start.6 = (s32[1,56,768]{2,1,0:T(8,128)S(1)}, s32[1,56,768]{2,1,0:T(8,128)}, u32[]{:S(2)}) copy-start(s32[1,56,768]{2,1,0:T(8,128)} %param.11) | copy-start | bytes 516100
  8.6 10.5 %copy-start.7 = (bf16[1,56,768]{2,1,0:T(8,128)(2,1)S(1)}, bf16[1,56,768]{2,1,0:T(8,128)(2,1)}, u32[]{:S(2)}) copy-start(bf16[1,56,768]{2,1,0:T(8,128)(2,1)} %param.12) | copy-start | bytes 258052
  8.6 82.6 %all-to-all-start = ((bf16[96,128,256]{2,1,0:T(8,128)(2,1)}), bf16[96,128,256]{2,1,0:T(8,128)(2,1)}, u32[]{:S(2)}, u32[]{:S(2)}) async-start(bf16[96,128,256]{2,1,0:T(8,128)(2,1)} %copy-done.1), calls=%async_computation | async-start | bytes 12582912 | tf_op jit(solution)/shard_map/all_to_all | solution.py:587
  25.2 1.5 copy-start.3
  91.2 78.3 %copy-start.8 = (f32[256,256]{1,0:T(8,128)S(1)}, f32[256,256]{1,0:T(8,128)}, u32[]{:S(2)}) copy-start(f32[256,256]{1,0:T(8,128)} %prior.1) | copy-start | bytes 786436
  91.2 78.3 %copy-start.9 = (f32[256]{0:T(256)S(1)}, f32[256]{0:T(256)}, u32[]{:S(2)}) copy-start(f32[256]{0:T(256)} %param.15) | copy-start | bytes 3076
  169.5 1.5 copy-start.5
  226.0 1.8 copy-start.2

commit v7 on v6

--- a/solution.py
+++ b/solution.py
@@ -461,56 +461,92 @@
     )(packed, noise.T, prior, shift.reshape(1, rank))
 
 
-def share_kernel(own, out, first_send, first_recv, send_sem, recv_sem, twin_send, twin_recv):
+def share_kernel(own, out, first_send, first_recv, x_send, x_recv, z_send, z_recv, twin_send, twin_recv):
     g, u = lax.axis_index("grp"), lax.axis_index("usr")
     ring, side = 4, 4
     core, x, z = u % 2, u // 2 % side, u // (2 * side)
     twin = u + 1 - 2 * core
-    moves = [(a, b) for a in range(side) for b in range(side) if a or b]
+    cut = ring // 2
 
     def place(dz, dx):
-        return (z + dz) % side * (2 * side) + (x + dx) % side * 2 + core
+        return (z + dz + side) % side * (2 * side) + (x + dx + side) % side * 2 + core
 
     barrier = pltpu.get_barrier_semaphore()
     for o in range(1, ring):
         pl.semaphore_signal(barrier, inc=1, device_id={"grp": (g + o) % ring}, device_id_type=MESH)
-    for move in moves:
-        pl.semaphore_signal(barrier, inc=1, device_id={"usr": place(*move)}, device_id_type=MESH)
-    pl.semaphore_signal(barrier, inc=1, device_id={"usr": twin}, device_id_type=MESH)
-    pl.semaphore_wait(barrier, ring + len(moves))
+    for peer in (place(0, 1), place(0, -1), place(1, 0), place(-1, 0), twin):
+        pl.semaphore_signal(barrier, inc=1, device_id={"usr": peer}, device_id_type=MESH)
+    pl.semaphore_wait(barrier, ring - 1 + 5)
+
+    started = []
 
     def remote(src, dst, send, recv, peer):
         return pltpu.make_async_remote_copy(
             src_ref=src, dst_ref=dst, send_sem=send, recv_sem=recv, device_id=peer, device_id_type=MESH
         )
 
-    first = [
-        remote(own, out.at[u, g], first_send.at[o - 1], first_recv.at[o - 1], {"grp": (g + o) % ring})
-        for o in range(1, ring)
-    ]
-    for c in first:
+    def send(slab, sems, k, peer):
+        c = remote(slab, slab, sems[0].at[k], sems[1].at[k], {"usr": peer})
         c.start()
+        started.append(c)
+
+    def wait(slab, sems, k):
+        remote(slab, slab, sems[0].at[k], sems[1].at[k], {"usr": twin}).wait_recv()
+
+    x_sems, z_sems, twin_sems = (x_send, x_recv), (z_send, z_recv), (twin_send, twin_recv)
+    twins = []
+
+    def to_twin(dz, dx):
+        k = len(twins)
+        twins.append(k)
+        send(out.at[place(dz, dx)], twin_sems, k, twin)
+
+    for o in range(1, ring):
+        c = remote(own, out.at[u, g], first_send.at[o - 1], first_recv.at[o - 1], {"grp": (g + o) % ring})
+        c.start()
+        started.append(c)
     out[u, g] = own[...]
     for o in range(1, ring):
         src = (g + ring - o) % ring
         remote(own, out.at[u, src], first_send.at[o - 1], first_recv.at[o - 1], {"grp": src}).wait_recv()
-    slab = out.at[u]
-    second = [
-        remote(slab, slab, send_sem.at[k], recv_sem.at[k], {"usr": place(*move)}) for k, move in enumerate(moves)
-    ]
-    for c in second:
-        c.start()
-    to_twin = [remote(slab, slab, twin_send.at[len(moves)], twin_recv.at[len(moves)], {"usr": twin})]
-    to_twin[0].start()
-    for k, (dz, dx) in enumerate(moves):
-        src = out.at[place(-dz + side, -dx + side)]
-        remote(src, src, send_sem.at[k], recv_sem.at[k], {"usr": twin}).wait_recv()
-        c = remote(src, src, twin_send.at[k], twin_recv.at[k], {"usr": twin})
-        c.start()
-        to_twin.append(c)
-    for c in to_twin:
-        c.wait_recv()
-    for c in first + second + to_twin:
+
+    columns = (0, -1, 1, 2)
+
+    def along_z(i):
+        slab = out.at[place(0, columns[i])]
+        send(slab, z_sems, 4 * i, place(1, 0))
+        send(slab, z_sems, 4 * i + 1, place(-1, 0))
+
+    send(out.at[u], x_sems, 0, place(0, 1))
+    send(out.at[u], x_sems, 1, place(0, -1))
+    along_z(0)
+    to_twin(0, 0)
+    wait(out.at[place(0, -1)], x_sems, 0)
+    send(out.at[place(0, -1), :cut], x_sems, 2, place(0, 1))
+    along_z(1)
+    wait(out.at[place(0, 1)], x_sems, 1)
+    send(out.at[place(0, 1), cut:], x_sems, 3, place(0, -1))
+    along_z(2)
+    to_twin(0, -1)
+    to_twin(0, 1)
+    wait(out.at[place(0, 2), :cut], x_sems, 2)
+    wait(out.at[place(0, 2), cut:], x_sems, 3)
+    along_z(3)
+    to_twin(0, 2)
+    for i, dx in enumerate(columns):
+        wait(out.at[place(-1, dx)], z_sems, 4 * i)
+        send(out.at[place(-1, dx), :cut], z_sems, 4 * i + 2, place(1, 0))
+        wait(out.at[place(1, dx)], z_sems, 4 * i + 1)
+        send(out.at[place(1, dx), cut:], z_sems, 4 * i + 3, place(-1, 0))
+        to_twin(-1, dx)
+        to_twin(1, dx)
+    for i, dx in enumerate(columns):
+        wait(out.at[place(2, dx), :cut], z_sems, 4 * i + 2)
+        wait(out.at[place(2, dx), cut:], z_sems, 4 * i + 3)
+        to_twin(2, dx)
+    for k in twins:
+        wait(out.at[u], twin_sems, k)
+    for c in started:
         c.wait_send()
 
 
@@ -524,7 +560,7 @@
         in_specs=[vmem],
         out_specs=vmem,
         out_shape=jax.ShapeDtypeStruct((peers, ring, share, rank), F32),
-        scratch_shapes=[dma((ring - 1,)), dma((ring - 1,)), dma((15,)), dma((15,)), dma((16,)), dma((16,))],
+        scratch_shapes=[dma((n,)) for n in (3, 3, 4, 4, 16, 16, 16, 16)],
         compiler_params=pltpu.CompilerParams(vmem_limit_bytes=32 * MIB, collective_id=1, has_side_effects=True),
         name="share_samples",
     )(own)

time: 234 us -> 233 us (level)
  no operation moved by 1% of the time
where the time goes in v7:
time: 233 us; the launch traced here: 232 us
  Pallas kernels  145 us (62%)
  waiting for transfers between devices  63.8 us (27%)
  local copies, waits for them, and re-layouts  11.5 us (5%)
  starting transfers between devices  9.61 us (4%)
    pallas_call x1, Pallas kernels, gram_terms(): pl.pallas_call(gram_kernel, in_specs=[pl.BlockSpec(memory_space=pltpu.SME...  78.3 us
    all_to_all x1, waiting for transfers between devices, on_device(): lax.all_to_all(outgoing, 'usr', split_axis=0, concat_axis=0, tiled=True)  63.8 us
    pallas_call x1, Pallas kernels, solve_users(): pl.pallas_call(solve_kernel, in_specs=[vmem] * 4, out_specs=vmem, out_sha...  28.2 us
    pallas_call x1, Pallas kernels, share_samples(): pl.pallas_call(share_kernel, in_specs=[vmem], out_specs=vmem, out_shape=j...  24.3 us
    unnamed x22, local copies, waits for them, and re-layouts  9.96 us
    all_to_all x1, starting transfers between devices, on_device(): lax.all_to_all(outgoing, 'usr', split_axis=0, concat_axis=0, tiled=True)  9.61 us
    pallas_call x1, Pallas kernels, make_stats(): pl.pallas_call(functools.partial(stats_kernel, n // peers), in_specs=[sme...  6.31 us
    pallas_call x1, Pallas kernels, make_weights(): pl.pallas_call(weight_kernel, grid=(users // group,), in_specs=[pl.BlockS...  6.1 us
  transfers between devices with their start and end apart: 1, of which 1 were waited for; matrix products, arithmetic and copies ran while one was open for 1% of the time, Pallas kernels for 3%

profile of v7, /device:TPU:1, one launch (start us, length us, event | category | flops | bytes accessed | tf_op | source)
XLA Modules:
  0.0 232.3 jit_solution(12686356578432358852)
XLA Ops:
  0.6 0.0 copy-start
  0.6 0.8 copy.12
  1.4 0.1 reshape_squeeze.3.listed
  1.5 0.7 fusion
  2.3 0.1 reshape.28.live
  2.4 0.0 copy-start.4
  2.4 1.6 copy-done.4
  4.0 2.0 pick_blocks.1
  5.9 0.0 copy-start.1
  6.0 2.6 %copy-done.1 = bf16[96,128,256]{2,1,0:T(8,128)(2,1)} copy-done((bf16[96,128,256]{2,1,0:T(8,128)(2,1)}, bf16[96,128,256]{2,1,0:T(8,128)(2,1)S(1)}, u32[]{:S(2)}) %copy-start.1) | copy-done | bytes 6291480
  8.6 0.0 copy-start.6
  8.6 9.6 %all-to-all-start = ((bf16[96,128,256]{2,1,0:T(8,128)(2,1)}), bf16[96,128,256]{2,1,0:T(8,128)(2,1)}, u32[]{:S(2)}, u32[]{:S(2)}) async-start(bf16[96,128,256]{2,1,0:T(8,128)(2,1)} %copy-done.1), calls=%async_computation | async-start | bytes 12582912 | tf_op jit(solution)/shard_map/all_to_all | solution.py:623
  18.2 0.0 copy-done.6
  18.2 0.7 mul.15.refs
  18.9 0.0 copy-done
  18.9 0.1 copy.14
  19.1 0.0 copy-done.7
  19.1 6.1 %make_weights.1.weights = f32[96,56,128]{2,1,0:T(8,128)S(1)} custom-call(s32[56,768]{1,0:T(8,128)S(1)} %bitcast.12, bf16[56,768]{1,0:T(8,128)(2,1)S(1)} %bitcast.14), custom_call_target="tpu_custom_call" | custom-call | tf_op jit(solution)/shard_map/make_weights/pallas_call | solution.py:91
  25.2 0.0 copy-start.3
  25.2 1.5 copy-done.3
  26.7 0.7 bitcast_convert_fusion.values
  27.4 63.8 %all-to-all-done = bf16[96,128,256]{2,1,0:T(8,128)(2,1)} async-done(((bf16[96,128,256]{2,1,0:T(8,128)(2,1)}), bf16[96,128,256]{2,1,0:T(8,128)(2,1)}, u32[]{:S(2)}, u32[]{:S(2)}) %all-to-all-start) | async-done | bytes 6291488 | tf_op jit(solution)/shard_map/all_to_all | solution.py:623
  91.2 78.3 %gram_terms.1 = (f32[14,264,128]{2,1,0:T(8,128)}, f32[96,56,128]{2,1,0:T(8,128)}) custom-call(s32[43008]{0:T(1024)} %mul.15.refs, bf16[12288,256]{1,0:T(8,128)(2,1)} %bitcast.2.table, f32[56,768]{1,0:T(8,128)} %bitcast_convert_fusion.values, f32[96,56,128]{2,1,0:T(8,128)} %copy-done.3), custom_call_target="tpu_custom_call" | custom-call | flops 60000002048 | bytes 209715200 | tf_op jit(solution)/shard_map/gram_terms/pallas_call | solution.py:296
  169.5 0.0 copy-done.8
  169.5 0.0 copy-done.9
  169.5 0.0 copy-start.5
  169.5 1.5 copy-done.5
  171.0 28.2 %solve_users.1.own = f32[14,256]{1,0:T(8,128)S(1)} custom-call(f32[14,264,128]{2,1,0:T(8,128)S(1)} %copy-done.5, f32[256,14]{1,0:T(8,128)S(1)} %bitcast.13, f32[256,256]{1,0:T(8,128)S(1)} %copy-done.8, f32[1,256]{1,0:T(1,128)S(1)} %bitcast.15), custom_call_target="tpu_custom_call" | custom-call | tf_op jit(solution)/shard_map/solve_users/pallas_call | solution.py:448
  199.2 24.3 %share_samples.1.samples = f32[32,4,14,256]{3,2,1,0:T(8,128)S(1)} custom-call(f32[14,256]{1,0:T(8,128)S(1)} %solve_users.1.own), custom_call_target="tpu_custom_call" | custom-call | tf_op jit(solution)/shard_map/share_samples/pallas_call | solution.py:558
  223.6 0.6 reshape.27
  224.2 1.8 copy-done.2
  226.0 6.3 %make_stats.1 = f32[32,128,256]{2,1,0:T(8,128)} custom-call(s32[96]{0:T(128)S(1)} %reshape_squeeze.3.listed, s32[96]{0:T(128)S(1)} %reshape.28.live, f32[96,56,128]{2,1,0:T(8,128)S(1)} %copy-done.2, f32[32,4,14,256]{3,2,1,0:T(8,128)S(1)} %share_samples.1.samples), custom_call_target="tpu_custom_call" | custom-call | tf_op jit(solution)/shard_map/make_stats/pallas_call | solution.py:601
  (7 shorter events, 0.0 us)
Async XLA Ops:
  0.6 18.3 %copy-start = (f32[56,256]{1,0:T(8,128)S(1)}, f32[56,256]{1,0:T(8,128)}, u32[]{:S(2)}) copy-start(f32[56,256]{1,0:T(8,128)} %param.13) | copy-start | bytes 172036
  2.4 1.6 copy-start.4
  5.9 2.6 %copy-start.1 = (bf16[96,128,256]{2,1,0:T(8,128)(2,1)}, bf16[96,128,256]{2,1,0:T(8,128)(2,1)S(1)}, u32[]{:S(2)}) copy-start(bf16[96,128,256]{2,1,0:T(8,128)(2,1)S(1)} %pick_blocks.1) | copy-start | bytes 18874372
  8.6 9.6 %copy-start.6 = (s32[1,56,768]{2,1,0:T(8,128)S(1)}, s32[1,56,768]{2,1,0:T(8,128)}, u32[]{:S(2)}) copy-start(s32[1,56,768]{2,1,0:T(8,128)} %param.11) | copy-start | bytes 516100
  8.6 10.5 %copy-start.7 = (bf16[1,56,768]{2,1,0:T(8,128)(2,1)S(1)}, bf16[1,56,768]{2,1,0:T(8,128)(2,1)}, u32[]{:S(2)}) copy-start(bf16[1,56,768]{2,1,0:T(8,128)(2,1)} %param.12) | copy-start | bytes 258052
  8.6 82.6 %all-to-all-start = ((bf16[96,128,256]{2,1,0:T(8,128)(2,1)}), bf16[96,128,256]{2,1,0:T(8,128)(2,1)}, u32[]{:S(2)}, u32[]{:S(2)}) async-start(bf16[96,128,256]{2,1,0:T(8,128)(2,1)} %copy-done.1), calls=%async_computation | async-start | bytes 12582912 | tf_op jit(solution)/shard_map/all_to_all | solution.py:623
  25.2 1.5 copy-start.3
  91.2 78.3 %copy-start.8 = (f32[256,256]{1,0:T(8,128)S(1)}, f32[256,256]{1,0:T(8,128)}, u32[]{:S(2)}) copy-start(f32[256,256]{1,0:T(8,128)} %prior.1) | copy-start | bytes 786436
  91.2 78.3 %copy-start.9 = (f32[256]{0:T(256)S(1)}, f32[256]{0:T(256)}, u32[]{:S(2)}) copy-start(f32[256]{0:T(256)} %param.15) | copy-start | bytes 3076
  169.5 1.5 copy-start.5
  224.2 1.8 copy-start.2

commit v8 on v7

--- a/solution.py
+++ b/solution.py
@@ -173,7 +173,7 @@
         wide[pl.ds(i * 2 * chunk + 1, chunk, stride=2), :] = part[:, 128:]
         return carry
 
-    lax.fori_loop(0, rows // chunk, widen, 0)
+    lax.fori_loop(0, rows // chunk, widen, 0, unroll=4)
     pl.semaphore_wait(barrier, peers + 1)
 
     keep = pltpu.make_async_copy(

time: 233 us -> 233 us (level)
  no operation moved by 1% of the time
where the time goes in v8:
time: 233 us; the launch traced here: 232 us
  Pallas kernels  145 us (62%)
  waiting for transfers between devices  63.8 us (27%)
  local copies, waits for them, and re-layouts  11.5 us (5%)
  starting transfers between devices  9.61 us (4%)
    pallas_call x1, Pallas kernels, gram_terms(): pl.pallas_call(gram_kernel, in_specs=[pl.BlockSpec(memory_space=pltpu.SME...  78.5 us
    all_to_all x1, waiting for transfers between devices, on_device(): lax.all_to_all(outgoing, 'usr', split_axis=0, concat_axis=0, tiled=True)  63.8 us
    pallas_call x1, Pallas kernels, solve_users(): pl.pallas_call(solve_kernel, in_specs=[vmem] * 4, out_specs=vmem, out_sha...  28.2 us
    pallas_call x1, Pallas kernels, share_samples(): pl.pallas_call(share_kernel, in_specs=[vmem], out_specs=vmem, out_shape=j...  24.2 us
    unnamed x22, local copies, waits for them, and re-layouts  9.96 us
    all_to_all x1, starting transfers between devices, on_device(): lax.all_to_all(outgoing, 'usr', split_axis=0, concat_axis=0, tiled=True)  9.61 us
    pallas_call x1, Pallas kernels, make_stats(): pl.pallas_call(functools.partial(stats_kernel, n // peers), in_specs=[sme...  6.31 us
    pallas_call x1, Pallas kernels, make_weights(): pl.pallas_call(weight_kernel, grid=(users // group,), in_specs=[pl.BlockS...  6.1 us
  transfers between devices with their start and end apart: 1, of which 1 were waited for; matrix products, arithmetic and copies ran while one was open for 1% of the time, Pallas kernels for 3%

profile of v8, /device:TPU:1, one launch (start us, length us, event | category | flops | bytes accessed | tf_op | source)
XLA Modules:
  0.0 232.3 jit_solution(793214629721476077)
XLA Ops:
  0.6 0.0 copy-start
  0.6 0.8 copy.12
  1.4 0.1 reshape_squeeze.3.listed
  1.5 0.7 fusion
  2.3 0.1 reshape.28.live
  2.4 0.0 copy-start.4
  2.4 1.6 copy-done.4
  4.0 2.0 pick_blocks.1
  5.9 0.0 copy-start.1
  6.0 2.6 %copy-done.1 = bf16[96,128,256]{2,1,0:T(8,128)(2,1)} copy-done((bf16[96,128,256]{2,1,0:T(8,128)(2,1)}, bf16[96,128,256]{2,1,0:T(8,128)(2,1)S(1)}, u32[]{:S(2)}) %copy-start.1) | copy-done | bytes 6291480
  8.6 0.0 copy-start.6
  8.6 9.6 %all-to-all-start = ((bf16[96,128,256]{2,1,0:T(8,128)(2,1)}), bf16[96,128,256]{2,1,0:T(8,128)(2,1)}, u32[]{:S(2)}, u32[]{:S(2)}) async-start(bf16[96,128,256]{2,1,0:T(8,128)(2,1)} %copy-done.1), calls=%async_computation | async-start | bytes 12582912 | tf_op jit(solution)/shard_map/all_to_all | solution.py:623
  18.2 0.0 copy-done.6
  18.2 0.7 mul.15.refs
  18.9 0.0 copy-done
  18.9 0.1 copy.14
  19.1 0.0 copy-done.7
  19.1 6.1 %make_weights.1.weights = f32[96,56,128]{2,1,0:T(8,128)S(1)} custom-call(s32[56,768]{1,0:T(8,128)S(1)} %bitcast.12, bf16[56,768]{1,0:T(8,128)(2,1)S(1)} %bitcast.14), custom_call_target="tpu_custom_call" | custom-call | tf_op jit(solution)/shard_map/make_weights/pallas_call | solution.py:91
  25.2 0.0 copy-start.3
  25.2 1.5 copy-done.3
  26.7 0.7 bitcast_convert_fusion.values
  27.4 63.8 %all-to-all-done = bf16[96,128,256]{2,1,0:T(8,128)(2,1)} async-done(((bf16[96,128,256]{2,1,0:T(8,128)(2,1)}), bf16[96,128,256]{2,1,0:T(8,128)(2,1)}, u32[]{:S(2)}, u32[]{:S(2)}) %all-to-all-start) | async-done | bytes 6291488 | tf_op jit(solution)/shard_map/all_to_all | solution.py:623
  91.2 78.5 %gram_terms.1 = (f32[14,264,128]{2,1,0:T(8,128)}, f32[96,56,128]{2,1,0:T(8,128)}) custom-call(s32[43008]{0:T(1024)} %mul.15.refs, bf16[12288,256]{1,0:T(8,128)(2,1)} %bitcast.2.table, f32[56,768]{1,0:T(8,128)} %bitcast_convert_fusion.values, f32[96,56,128]{2,1,0:T(8,128)} %copy-done.3), custom_call_target="tpu_custom_call" | custom-call | flops 60000002048 | bytes 209715200 | tf_op jit(solution)/shard_map/gram_terms/pallas_call | solution.py:296
  169.7 0.0 copy-done.8
  169.7 0.0 copy-done.9
  169.7 0.0 copy-start.5
  169.7 1.5 copy-done.5
  171.2 28.2 %solve_users.1.own = f32[14,256]{1,0:T(8,128)S(1)} custom-call(f32[14,264,128]{2,1,0:T(8,128)S(1)} %copy-done.5, f32[256,14]{1,0:T(8,128)S(1)} %bitcast.13, f32[256,256]{1,0:T(8,128)S(1)} %copy-done.8, f32[1,256]{1,0:T(1,128)S(1)} %bitcast.15), custom_call_target="tpu_custom_call" | custom-call | tf_op jit(solution)/shard_map/solve_users/pallas_call | solution.py:448
  199.4 24.2 %share_samples.1.samples = f32[32,4,14,256]{3,2,1,0:T(8,128)S(1)} custom-call(f32[14,256]{1,0:T(8,128)S(1)} %solve_users.1.own), custom_call_target="tpu_custom_call" | custom-call | tf_op jit(solution)/shard_map/share_samples/pallas_call | solution.py:558
  223.6 0.6 reshape.27
  224.2 1.8 copy-done.2
  226.0 6.3 %make_stats.1 = f32[32,128,256]{2,1,0:T(8,128)} custom-call(s32[96]{0:T(128)S(1)} %reshape_squeeze.3.listed, s32[96]{0:T(128)S(1)} %reshape.28.live, f32[96,56,128]{2,1,0:T(8,128)S(1)} %copy-done.2, f32[32,4,14,256]{3,2,1,0:T(8,128)S(1)} %share_samples.1.samples), custom_call_target="tpu_custom_call" | custom-call | tf_op jit(solution)/shard_map/make_stats/pallas_call | solution.py:601
  (7 shorter events, 0.0 us)
Async XLA Ops:
  0.6 18.3 %copy-start = (f32[56,256]{1,0:T(8,128)S(1)}, f32[56,256]{1,0:T(8,128)}, u32[]{:S(2)}) copy-start(f32[56,256]{1,0:T(8,128)} %param.13) | copy-start | bytes 172036
  2.4 1.6 copy-start.4
  5.9 2.6 %copy-start.1 = (bf16[96,128,256]{2,1,0:T(8,128)(2,1)}, bf16[96,128,256]{2,1,0:T(8,128)(2,1)S(1)}, u32[]{:S(2)}) copy-start(bf16[96,128,256]{2,1,0:T(8,128)(2,1)S(1)} %pick_blocks.1) | copy-start | bytes 18874372
  8.6 9.6 %copy-start.6 = (s32[1,56,768]{2,1,0:T(8,128)S(1)}, s32[1,56,768]{2,1,0:T(8,128)}, u32[]{:S(2)}) copy-start(s32[1,56,768]{2,1,0:T(8,128)} %param.11) | copy-start | bytes 516100
  8.6 10.5 %copy-start.7 = (bf16[1,56,768]{2,1,0:T(8,128)(2,1)S(1)}, bf16[1,56,768]{2,1,0:T(8,128)(2,1)}, u32[]{:S(2)}) copy-start(bf16[1,56,768]{2,1,0:T(8,128)(2,1)} %param.12) | copy-start | bytes 258052
  8.6 82.6 %all-to-all-start = ((bf16[96,128,256]{2,1,0:T(8,128)(2,1)}), bf16[96,128,256]{2,1,0:T(8,128)(2,1)}, u32[]{:S(2)}, u32[]{:S(2)}) async-start(bf16[96,128,256]{2,1,0:T(8,128)(2,1)} %copy-done.1), calls=%async_computation | async-start | bytes 12582912 | tf_op jit(solution)/shard_map/all_to_all | solution.py:623
  25.2 1.5 copy-start.3
  91.2 78.5 %copy-start.8 = (f32[256,256]{1,0:T(8,128)S(1)}, f32[256,256]{1,0:T(8,128)}, u32[]{:S(2)}) copy-start(f32[256,256]{1,0:T(8,128)} %prior.1) | copy-start | bytes 786436
  91.2 78.5 %copy-start.9 = (f32[256]{0:T(256)S(1)}, f32[256]{0:T(256)}, u32[]{:S(2)}) copy-start(f32[256]{0:T(256)} %param.15) | copy-start | bytes 3076
  169.7 1.5 copy-start.5
  224.2 1.8 copy-start.2
